TPU v7x, 128 devices: a whole 4x4x4 slice. The times are simulated.
128 devices in a mesh: segment: 4 (over x), seq: 16 (over z, y), mp: 2 (over core).
Axes of the slice: x: 4, y: 4, z: 4, core: 2. Of those that a mesh axis runs over, the one named last changes fastest.
Arguments:
- video: bfloat16 [3, 1024, 6144], P(None, 'seq', 'mp'), may hold values from -6 to 6
- caption_kv: bfloat16 [4, 768, 2, 3072], P('segment', 'seq', None, 'mp'), may hold values from -6 to 6
- caption_lengths: int32 [3], replicated, may hold values from 1 to 400, 768 in all
- order: int32 [3], replicated, may hold values from 0 to 2, each once
- gains: float32 [4, 6144], P('segment'), may hold values from 0.25 to 1.75
- w_query: bfloat16 [4, 6144, 3072], P('segment', 'seq', 'mp')
- w_out: bfloat16 [4, 3072, 6144], P('segment', None, 'mp'), may hold values from -0.109375 to 0.109375
Outputs:
- section_out: bfloat16 [4, 3, 1024, 6144], P('segment', None, 'seq', 'mp')
Inputs may be any that keep to these rules, and one draw needn't show every extreme that they name: `caption_lengths`: caption lengths sum to 768; the largest is exactly 400. `order`: each sample is named by exactly one micro-batch.
All inputs are finite; a program needn't handle non-finite values.
Results may differ from a plain program's by a relative error of at most 0.009.
Values may be sent and summed in bfloat16 or wider, within the bound.
No kernel may reach another device: no remote copies, remote signals or barrier semaphores. Data moves between devices by JAX's collectives and lax.ppermute only.
A program may use at most 128 MiB of HBM per device.

v0:
```python
import jax
import jax.numpy as jnp
from jax import lax
from jax.sharding import PartitionSpec as P

HEAD_DIM = 128


def passed_along(block, axis, distance):
    devices = range(lax.axis_size(axis))
    route = [(i - distance, i) for i in devices if i - distance in devices]
    return lax.ppermute(block, axis, route)


def block_terms(query, kv, start_row, length):
    tokens = query.shape[0]
    heads = query.shape[1] // HEAD_DIM
    count = kv.shape[0]
    qheads = query.reshape(tokens, heads, HEAD_DIM)
    keys = kv[:, 0, :].reshape(count, heads, HEAD_DIM)
    values = kv[:, 1, :].astype(jnp.float32).reshape(count, heads, HEAD_DIM)
    scores = jnp.einsum(
        "thd,rhd->htr", qheads, keys, preferred_element_type=jnp.float32
    ) * HEAD_DIM ** (-0.5)
    rows = jnp.arange(count, dtype=jnp.int32)
    valid = (rows >= start_row) & (rows < start_row + length)
    scores = jnp.where(valid[None, None, :], scores, -1e30)
    top = jnp.max(scores, axis=-1)
    weights = jnp.where(valid[None, None, :], jnp.exp(scores - top[:, :, None]), 0.0)
    total = jnp.sum(weights, axis=-1)
    acc = jnp.einsum("htr,rhd->htd", weights, values)
    return (top, total, acc)


def finish(total, acc):
    heads, tokens, width = acc.shape
    result = acc / total[:, :, None]
    return jnp.transpose(result, (1, 0, 2)).reshape(tokens, heads * width).astype(jnp.bfloat16)


def body(video, caption_kv, caption_lengths, order, gains, w_query, w_out):
    samples = video.shape[0]
    segments = lax.axis_size("segment")
    here = lax.axis_index("segment")
    gain = gains[0]
    w_local = w_query[0]
    out_weight = w_out[0]
    kv_local = caption_kv[0]
    offsets = jnp.cumsum(caption_lengths) - caption_lengths
    w_whole = lax.all_gather(w_local, "seq", axis=0, tiled=True)
    kv_whole = lax.all_gather(kv_local, "seq", axis=0, tiled=True)
    received = jnp.zeros_like(video[0])
    section_out = jnp.zeros_like(video)
    for tick in range(samples + segments - 1):
        micro = tick - here
        active = (micro >= 0) & (micro < samples)
        slot = jnp.clip(micro, 0, samples - 1)
        sample = order[slot]
        first = lax.dynamic_index_in_dim(video, sample, 0, keepdims=False)
        current = jnp.where(here == 0, first, received)
        whole = lax.all_gather(current, "mp", axis=1, tiled=True)
        wholef = whole.astype(jnp.float32)
        meansq = jnp.mean(wholef * wholef, axis=-1, keepdims=True)
        normed = (wholef * lax.rsqrt(meansq + 1e-06) * gain).astype(jnp.bfloat16)
        query = jnp.dot(normed, w_whole, preferred_element_type=jnp.float32)
        query = query.astype(jnp.bfloat16)
        start_row = offsets[sample]
        length = caption_lengths[sample]
        top, total, acc = block_terms(query, kv_whole, start_row, length)
        attended = finish(total, acc)
        projected = jnp.dot(
            lax.all_gather(attended, "mp", axis=1, tiled=True),
            out_weight,
            preferred_element_type=jnp.float32,
        )
        mixed = (current.astype(jnp.float32) + projected).astype(jnp.bfloat16)
        updated = lax.dynamic_update_index_in_dim(section_out, mixed, slot, 0)
        section_out = jnp.where(active, updated, section_out)
        received = passed_along(mixed, "segment", 1)
    return section_out[None]


def solution(mesh):
    in_specs = (
        P(None, "seq", "mp"),
        P("segment", "seq", None, "mp"),
        P(),
        P(),
        P("segment", None),
        P("segment", "seq", "mp"),
        P("segment", None, "mp"),
    )
    out_specs = P("segment", None, "seq", "mp")
    return jax.shard_map(body, mesh=mesh, in_specs=in_specs, out_specs=out_specs, check_vma=False)
```

profile of v0, /device:TPU:3, one launch (start us, length us, event | category | flops | bytes accessed | tf_op | source)
XLA Modules:
  0.0 404.3 jit_solution(10099072655989508050)
XLA Ops:
  28.0 2.7 all-gather
  30.9 35.1 %all-gather.8.cloned.1.call-done = bf16[1,768,2,1536]{3,2,0,1:T(2,128)(2,1)} async-done(((bf16[1,48,2,1536]{3,2,0,1:T(2,128)(2,1)}), bf16[1,768,2,1536]{3,2,0,1:T(2,128)(2,1)}) %all-gather.8.cloned.1.call-update) | async-done | bytes 4718608 | tf_op jit(solution)/shard_map/all_gather | solution.py:51
  66.0 12.5 %copy.40 = bf16[1,768,2,1536]{1,3,2,0:T(8,128)(2,1)} copy(bf16[1,768,2,1536]{3,2,0,1:T(2,128)(2,1)} %all-gather.8.cloned.1.call-done) | data formatting | bytes 9437184 | tf_op jit(solution)/shard_map/all_gather | solution.py:51
  78.5 4.7 %fusion.225 = (bf16[768,1,1536]{0,2,1:T(8,128)(2,1)S(1)}, bf16[768,1,1536]{0,2,1:T(8,128)(2,1)}) fusion(bf16[768,2,1536]{0,2,1:T(8,128)(2,1)} %bitcast.305), kind=kLoop, calls=%fused_computation.256 | loop fusion | bytes 9437184 | tf_op jit(solution)/shard_map/slice | solution.py:20
  83.1 106.8 %all-gather.6.cloned.1.call-done = bf16[1,6144,1536]{2,1,0:T(8,128)(2,1)} async-done(((bf16[1,384,1536]{2,1,0:T(8,128)(2,1)}), bf16[1,6144,1536]{2,1,0:T(8,128)(2,1)}) %all-gather.6.cloned.1.call-update) | async-done | bytes 18874384 | tf_op jit(solution)/shard_map/all_gather | solution.py:50
  189.9 10.0 %fusion.135 = bf16[8,12,8,128]{3,2,1,0:T(8,128)(2,1)S(1)} fusion(bf16[1,6144,1536]{2,1,0:T(8,128)(2,1)} %all-gather.6.cloned.1.call-done, bf16[1,64,6144]{2,1,0:T(8,128)(2,1)S(1)} %all-gather, f32[6144]{0:T(1024)S(1)} %bitcast.307, f32[64]{0:T(128)S(1)} %add_rsqrt_fusion.5), kind=kOutput, calls=%fused_computation.133 | convolution fusion | flops 1209630720 | bytes 19882240 | tf_op jit(solution)/shard_map/dot_general | solution.py:65
  206.1 4.2 %bitcast_dynamic-update-slice_fusion = (bf16[3,64,3072]{2,1,0:T(8,128)(2,1)S(1)}, bf16[64,3072]{1,0:T(8,128)(2,1)}) fusion(bf16[3,64,3072]{2,1,0:T(8,128)(2,1)S(1)} %broadcast_in_dim.128, s32[]{:T(128)S(6)} %min.19, pred[]{:T(512)S(6)} %and.61, bf16[64,3072]{1,0:T(8,128)(2,1)S(1)} %all_gather.45, bf16[1,3072,3072]{2,1,0:T(8,128)(2,1)S(1)} %bitcast.288, ...), kind=kOutput, calls=%fused_computation.187 | convolution fusion | flops 1208745984 | bytes 20447236 | tf_op jit(solution)/shard_map/dot_general | solution.py:71
  210.4 3.1 collective-permute-start
  215.2 7.7 %collective-permute-done = bf16[64,3072]{1,0:T(8,128)(2,1)} collective-permute-done((bf16[64,3072]{1,0:T(8,128)(2,1)}, bf16[64,3072]{1,0:T(8,128)(2,1)}, u32[]{:S(2)}, u32[]{:S(2)}) %collective-permute-start) | collective-permute-done | bytes 393248 | tf_op jit(solution)/shard_map/ppermute | solution.py:12
  224.1 3.4 all_gather.46
  227.8 10.0 %fusion.132 = bf16[8,12,8,128]{3,2,1,0:T(8,128)(2,1)S(1)} fusion(bf16[1,6144,1536]{2,1,0:T(8,128)(2,1)} %all-gather.6.cloned.1.call-done, bf16[64,6144]{1,0:T(8,128)(2,1)S(1)} %all_gather.46, f32[64]{0:T(128)S(1)} %add_rsqrt_fusion.4, f32[6144]{0:T(1024)S(1)} %bitcast.308), kind=kOutput, calls=%fused_computation.132 | convolution fusion | flops 1209630720 | bytes 19882240 | tf_op jit(solution)/shard_map/dot_general | solution.py:65
  243.4 4.3 %fusion.182 = (bf16[3,64,3072]{2,1,0:T(8,128)(2,1)S(1)}, bf16[64,3072]{1,0:T(8,128)(2,1)}) fusion(bf16[3,64,3072]{2,1,0:T(8,128)(2,1)S(1)} %get-tuple-element.35, s32[]{:T(128)S(6)} %min.20, pred[]{:T(512)S(6)} %and.63, bf16[64,3072]{1,0:T(8,128)(2,1)S(1)} %bitcast_select_fusion.8, bf16[64,3072]{1,0:T(8,128)(2,1)S(1)} %all_gather.47, ...), kind=kOutput, calls=%fused_computation.185 | convolution fusion | flops 1208745984 | bytes 20840452 | tf_op jit(solution)/shard_map/dot_general | solution.py:71
  247.7 3.1 collective-permute-start.1
  252.7 7.5 %collective-permute-done.1 = bf16[64,3072]{1,0:T(8,128)(2,1)} collective-permute-done((bf16[64,3072]{1,0:T(8,128)(2,1)}, bf16[64,3072]{1,0:T(8,128)(2,1)}, u32[]{:S(2)}, u32[]{:S(2)}) %collective-permute-start.1) | collective-permute-done | bytes 393248 | tf_op jit(solution)/shard_map/ppermute | solution.py:12
  261.4 3.4 all_gather.48
  265.2 10.0 %fusion.129 = bf16[8,12,8,128]{3,2,1,0:T(8,128)(2,1)S(1)} fusion(bf16[1,6144,1536]{2,1,0:T(8,128)(2,1)} %all-gather.6.cloned.1.call-done, bf16[64,6144]{1,0:T(8,128)(2,1)S(1)} %all_gather.48, f32[64]{0:T(128)S(1)} %add_rsqrt_fusion.3, f32[6144]{0:T(1024)S(1)} %bitcast.309), kind=kOutput, calls=%fused_computation.131 | convolution fusion | flops 1209630720 | bytes 19882240 | tf_op jit(solution)/shard_map/dot_general | solution.py:65
  280.8 4.3 %fusion.181 = (bf16[3,64,3072]{2,1,0:T(8,128)(2,1)S(1)}, bf16[64,3072]{1,0:T(8,128)(2,1)}) fusion(bf16[3,64,3072]{2,1,0:T(8,128)(2,1)S(1)} %get-tuple-element.11, s32[]{:T(128)S(6)} %min.21, pred[]{:T(512)S(6)} %and.65, bf16[64,3072]{1,0:T(8,128)(2,1)S(1)} %bitcast_select_fusion.6, bf16[64,3072]{1,0:T(8,128)(2,1)S(1)} %all_gather.49, ...), kind=kOutput, calls=%fused_computation.182 | convolution fusion | flops 1208745984 | bytes 20840452 | tf_op jit(solution)/shard_map/dot_general | solution.py:71
  285.1 3.1 collective-permute-start.2
  290.1 7.5 %collective-permute-done.2 = bf16[64,3072]{1,0:T(8,128)(2,1)} collective-permute-done((bf16[64,3072]{1,0:T(8,128)(2,1)}, bf16[64,3072]{1,0:T(8,128)(2,1)}, u32[]{:S(2)}, u32[]{:S(2)}) %collective-permute-start.2) | collective-permute-done | bytes 393248 | tf_op jit(solution)/shard_map/ppermute | solution.py:12
  298.7 3.7 all_gather.50
  302.7 10.0 %fusion.126 = bf16[8,12,8,128]{3,2,1,0:T(8,128)(2,1)S(1)} fusion(bf16[1,6144,1536]{2,1,0:T(8,128)(2,1)} %all-gather.6.cloned.1.call-done, bf16[64,6144]{1,0:T(8,128)(2,1)S(1)} %all_gather.50, f32[64]{0:T(128)S(1)} %add_rsqrt_fusion.2, f32[6144]{0:T(1024)S(1)} %bitcast.310), kind=kOutput, calls=%fused_computation.130 | convolution fusion | flops 1209630720 | bytes 19882240 | tf_op jit(solution)/shard_map/dot_general | solution.py:65
  318.4 4.3 %fusion.180 = (bf16[3,64,3072]{2,1,0:T(8,128)(2,1)S(1)}, bf16[64,3072]{1,0:T(8,128)(2,1)}) fusion(bf16[3,64,3072]{2,1,0:T(8,128)(2,1)S(1)} %get-tuple-element.9, s32[]{:T(128)S(6)} %min.22, pred[]{:T(512)S(6)} %and.67, bf16[64,3072]{1,0:T(8,128)(2,1)S(1)} %bitcast_select_fusion.4, bf16[64,3072]{1,0:T(8,128)(2,1)S(1)} %all_gather.51, ...), kind=kOutput, calls=%fused_computation.179 | convolution fusion | flops 1208745984 | bytes 20840452 | tf_op jit(solution)/shard_map/dot_general | solution.py:71
  322.6 3.1 collective-permute-start.3
  327.7 7.5 %collective-permute-done.3 = bf16[64,3072]{1,0:T(8,128)(2,1)} collective-permute-done((bf16[64,3072]{1,0:T(8,128)(2,1)}, bf16[64,3072]{1,0:T(8,128)(2,1)}, u32[]{:S(2)}, u32[]{:S(2)}) %collective-permute-start.3) | collective-permute-done | bytes 393248 | tf_op jit(solution)/shard_map/ppermute | solution.py:12
  336.3 3.4 all_gather.52
  340.0 10.0 %fusion.123 = bf16[8,12,8,128]{3,2,1,0:T(8,128)(2,1)S(1)} fusion(bf16[1,6144,1536]{2,1,0:T(8,128)(2,1)} %all-gather.6.cloned.1.call-done, bf16[64,6144]{1,0:T(8,128)(2,1)S(1)} %all_gather.52, f32[64]{0:T(128)S(1)} %add_rsqrt_fusion.1, f32[6144]{0:T(1024)S(1)} %bitcast.311), kind=kOutput, calls=%fused_computation.129 | convolution fusion | flops 1209630720 | bytes 19882240 | tf_op jit(solution)/shard_map/dot_general | solution.py:65
  355.6 4.3 %fusion.179 = (bf16[3,64,3072]{2,1,0:T(8,128)(2,1)S(1)}, bf16[64,3072]{1,0:T(8,128)(2,1)}) fusion(bf16[3,64,3072]{2,1,0:T(8,128)(2,1)S(1)} %get-tuple-element.7, s32[]{:T(128)S(6)} %min.23, pred[]{:T(512)S(6)} %and.69, bf16[64,3072]{1,0:T(8,128)(2,1)S(1)} %bitcast_select_fusion.2, bf16[64,3072]{1,0:T(8,128)(2,1)S(1)} %all_gather.53, ...), kind=kOutput, calls=%fused_computation.176 | convolution fusion | flops 1208745984 | bytes 20840452 | tf_op jit(solution)/shard_map/dot_general | solution.py:71
  359.9 3.1 collective-permute-start.4
  365.9 6.5 %collective-permute-done.4 = bf16[64,3072]{1,0:T(8,128)(2,1)} collective-permute-done((bf16[64,3072]{1,0:T(8,128)(2,1)}, bf16[64,3072]{1,0:T(8,128)(2,1)}, u32[]{:S(2)}, u32[]{:S(2)}) %collective-permute-start.4) | collective-permute-done | bytes 393248 | tf_op jit(solution)/shard_map/ppermute | solution.py:12
  373.6 3.4 all_gather.54
  377.3 10.0 %fusion.120 = bf16[8,12,8,128]{3,2,1,0:T(8,128)(2,1)S(1)} fusion(bf16[1,6144,1536]{2,1,0:T(8,128)(2,1)} %all-gather.6.cloned.1.call-done, bf16[64,6144]{1,0:T(8,128)(2,1)S(1)} %all_gather.54, f32[64]{0:T(128)S(1)} %add_rsqrt_fusion, f32[6144]{0:T(1024)S(1)} %bitcast.312), kind=kOutput, calls=%fused_computation.128 | convolution fusion | flops 1209630720 | bytes 19882240 | tf_op jit(solution)/shard_map/dot_general | solution.py:65
  393.0 4.3 %fusion.178 = bf16[1,3,64,3072]{3,2,1,0:T(8,128)(2,1)} fusion(bf16[1,3,64,3072]{3,2,1,0:T(8,128)(2,1)} %copy.142, s32[]{:T(128)S(6)} %min.24, bf16[64,3072]{1,0:T(8,128)(2,1)S(1)} %bitcast_select_fusion, bf16[3,64,3072]{2,1,0:T(8,128)(2,1)S(1)} %get-tuple-element.5, pred[]{:T(512)S(6)} %and.71, bf16[64,3072]{1,0:T(8,128)(2,1)S(1)} %all_gather.55, ...), kind=kOutput, calls=%fused_computation.173 | convolution fusion | flops 1208745984 | bytes 20447236 | tf_op jit(solution)/shard_map/dot_general | solution.py:71
  (158 shorter events, 54.1 us)
Async XLA Ops:
  6.5 59.5 %all-gather.8.cloned.1.call-start = ((), (), s32[]{:S(2)}) async-start(), calls=%async_computation.1 | async-start | bytes 5013504 | tf_op jit(solution)/shard_map/all_gather | solution.py:51
  7.3 182.7 %all-gather.6.cloned.1.call-start = ((), (), s32[]{:S(2)}) async-start(), calls=%async_computation | async-start | bytes 20054016 | tf_op jit(solution)/shard_map/all_gather | solution.py:50
  78.5 111.4 %copy-start = (f32[1,6144]{1,0:T(1,128)S(1)}, f32[1,6144]{1,0:T(1,128)}, u32[]{:S(2)}) copy-start(f32[1,6144]{1,0:T(1,128)} %param.11) | copy-start | bytes 73732
  189.9 16.2 %slice-start = ((s8[18874368]{0:T(1024)(128)(4,1)}), s8[4194304]{0:T(1024)(128)(4,1)S(1)}, s32[]{:S(2)}) async-start(s8[18874368]{0:T(1024)(128)(4,1)} %bitcast.287), calls=%async_computation.2 | async-start | bytes 8388608
  189.9 16.2 %slice-start.1 = ((s8[18874368]{0:T(1024)(128)(4,1)}), s8[4194304]{0:T(1024)(128)(4,1)S(1)}, s32[]{:S(2)}) async-start(s8[18874368]{0:T(1024)(128)(4,1)} %bitcast.287), calls=%async_computation.3 | async-start | bytes 8388608
  189.9 16.2 %slice-start.2 = ((s8[18874368]{0:T(1024)(128)(4,1)}), s8[4194304]{0:T(1024)(128)(4,1)S(1)}, s32[]{:S(2)}) async-start(s8[18874368]{0:T(1024)(128)(4,1)} %bitcast.287), calls=%async_computation.4 | async-start | bytes 8388608
  189.9 16.2 %slice-start.3 = ((s8[18874368]{0:T(1024)(128)(4,1)}), s8[4194304]{0:T(1024)(128)(4,1)S(1)}, s32[]{:S(2)}) async-start(s8[18874368]{0:T(1024)(128)(4,1)} %bitcast.287), calls=%async_computation.5 | async-start | bytes 8388608
  210.4 12.5 %collective-permute-start = (bf16[64,3072]{1,0:T(8,128)(2,1)}, bf16[64,3072]{1,0:T(8,128)(2,1)}, u32[]{:S(2)}, u32[]{:S(2)}) collective-permute-start(bf16[64,3072]{1,0:T(8,128)(2,1)} %get-tuple-element.36), channel_id=1, source_target_pairs={{0,32},{32,64},{64,96},{1,33},{33,65},{65,97},{2,34},{34,66},{66,9... | collective-permute-start | bytes 1179656 | tf_op jit(solution)/shard_map/ppermute | solution.py:12
  227.7 15.6 %slice-start.5 = ((s8[18874368]{0:T(1024)(128)(4,1)}), s8[4194304]{0:T(1024)(128)(4,1)S(1)}, s32[]{:S(2)}) async-start(s8[18874368]{0:T(1024)(128)(4,1)} %bitcast.289), calls=%async_computation.7 | async-start | bytes 8388608
  227.8 15.6 %slice-start.6 = ((s8[18874368]{0:T(1024)(128)(4,1)}), s8[4194304]{0:T(1024)(128)(4,1)S(1)}, s32[]{:S(2)}) async-start(s8[18874368]{0:T(1024)(128)(4,1)} %bitcast.289), calls=%async_computation.8 | async-start | bytes 8388608
  227.8 15.6 %slice-start.7 = ((s8[18874368]{0:T(1024)(128)(4,1)}), s8[4194304]{0:T(1024)(128)(4,1)S(1)}, s32[]{:S(2)}) async-start(s8[18874368]{0:T(1024)(128)(4,1)} %bitcast.289), calls=%async_computation.9 | async-start | bytes 8388608
  227.8 15.6 %slice-start.8 = ((s8[18874368]{0:T(1024)(128)(4,1)}), s8[4194304]{0:T(1024)(128)(4,1)S(1)}, s32[]{:S(2)}) async-start(s8[18874368]{0:T(1024)(128)(4,1)} %bitcast.289), calls=%async_computation.10 | async-start | bytes 8388608
  247.7 12.5 %collective-permute-start.1 = (bf16[64,3072]{1,0:T(8,128)(2,1)}, bf16[64,3072]{1,0:T(8,128)(2,1)}, u32[]{:S(2)}, u32[]{:S(2)}) collective-permute-start(bf16[64,3072]{1,0:T(8,128)(2,1)} %get-tuple-element.12), channel_id=1, source_target_pairs={{0,32},{32,64},{64,96},{1,33},{33,65},{65,97},{2,34},{34,66},{66,9... | collective-permute-start | bytes 1179656 | tf_op jit(solution)/shard_map/ppermute | solution.py:12
  265.1 15.6 %slice-start.10 = ((s8[18874368]{0:T(1024)(128)(4,1)}), s8[4194304]{0:T(1024)(128)(4,1)S(1)}, s32[]{:S(2)}) async-start(s8[18874368]{0:T(1024)(128)(4,1)} %bitcast.291), calls=%async_computation.12 | async-start | bytes 8388608
  265.1 15.6 %slice-start.11 = ((s8[18874368]{0:T(1024)(128)(4,1)}), s8[4194304]{0:T(1024)(128)(4,1)S(1)}, s32[]{:S(2)}) async-start(s8[18874368]{0:T(1024)(128)(4,1)} %bitcast.291), calls=%async_computation.13 | async-start | bytes 8388608
  265.1 15.6 %slice-start.12 = ((s8[18874368]{0:T(1024)(128)(4,1)}), s8[4194304]{0:T(1024)(128)(4,1)S(1)}, s32[]{:S(2)}) async-start(s8[18874368]{0:T(1024)(128)(4,1)} %bitcast.291), calls=%async_computation.14 | async-start | bytes 8388608
  265.1 15.6 %slice-start.13 = ((s8[18874368]{0:T(1024)(128)(4,1)}), s8[4194304]{0:T(1024)(128)(4,1)S(1)}, s32[]{:S(2)}) async-start(s8[18874368]{0:T(1024)(128)(4,1)} %bitcast.291), calls=%async_computation.15 | async-start | bytes 8388608
  285.1 12.5 %collective-permute-start.2 = (bf16[64,3072]{1,0:T(8,128)(2,1)}, bf16[64,3072]{1,0:T(8,128)(2,1)}, u32[]{:S(2)}, u32[]{:S(2)}) collective-permute-start(bf16[64,3072]{1,0:T(8,128)(2,1)} %get-tuple-element.10), channel_id=1, source_target_pairs={{0,32},{32,64},{64,96},{1,33},{33,65},{65,97},{2,34},{34,66},{66,9... | collective-permute-start | bytes 1179656 | tf_op jit(solution)/shard_map/ppermute | solution.py:12
  302.7 15.6 %slice-start.15 = ((s8[18874368]{0:T(1024)(128)(4,1)}), s8[4194304]{0:T(1024)(128)(4,1)S(1)}, s32[]{:S(2)}) async-start(s8[18874368]{0:T(1024)(128)(4,1)} %bitcast.293), calls=%async_computation.17 | async-start | bytes 8388608
  302.7 15.6 %slice-start.16 = ((s8[18874368]{0:T(1024)(128)(4,1)}), s8[4194304]{0:T(1024)(128)(4,1)S(1)}, s32[]{:S(2)}) async-start(s8[18874368]{0:T(1024)(128)(4,1)} %bitcast.293), calls=%async_computation.18 | async-start | bytes 8388608
  302.7 15.6 %slice-start.17 = ((s8[18874368]{0:T(1024)(128)(4,1)}), s8[4194304]{0:T(1024)(128)(4,1)S(1)}, s32[]{:S(2)}) async-start(s8[18874368]{0:T(1024)(128)(4,1)} %bitcast.293), calls=%async_computation.19 | async-start | bytes 8388608
  302.7 15.6 %slice-start.18 = ((s8[18874368]{0:T(1024)(128)(4,1)}), s8[4194304]{0:T(1024)(128)(4,1)S(1)}, s32[]{:S(2)}) async-start(s8[18874368]{0:T(1024)(128)(4,1)} %bitcast.293), calls=%async_computation.20 | async-start | bytes 8388608
  322.6 12.5 %collective-permute-start.3 = (bf16[64,3072]{1,0:T(8,128)(2,1)}, bf16[64,3072]{1,0:T(8,128)(2,1)}, u32[]{:S(2)}, u32[]{:S(2)}) collective-permute-start(bf16[64,3072]{1,0:T(8,128)(2,1)} %get-tuple-element.8), channel_id=1, source_target_pairs={{0,32},{32,64},{64,96},{1,33},{33,65},{65,97},{2,34},{34,66},{66,9... | collective-permute-start | bytes 1179656 | tf_op jit(solution)/shard_map/ppermute | solution.py:12
  340.0 15.6 %slice-start.20 = ((s8[18874368]{0:T(1024)(128)(4,1)}), s8[4194304]{0:T(1024)(128)(4,1)S(1)}, s32[]{:S(2)}) async-start(s8[18874368]{0:T(1024)(128)(4,1)} %bitcast.295), calls=%async_computation.22 | async-start | bytes 8388608
  340.0 15.6 %slice-start.21 = ((s8[18874368]{0:T(1024)(128)(4,1)}), s8[4194304]{0:T(1024)(128)(4,1)S(1)}, s32[]{:S(2)}) async-start(s8[18874368]{0:T(1024)(128)(4,1)} %bitcast.295), calls=%async_computation.23 | async-start | bytes 8388608
  340.0 15.6 %slice-start.22 = ((s8[18874368]{0:T(1024)(128)(4,1)}), s8[4194304]{0:T(1024)(128)(4,1)S(1)}, s32[]{:S(2)}) async-start(s8[18874368]{0:T(1024)(128)(4,1)} %bitcast.295), calls=%async_computation.24 | async-start | bytes 8388608
  340.0 15.6 %slice-start.23 = ((s8[18874368]{0:T(1024)(128)(4,1)}), s8[4194304]{0:T(1024)(128)(4,1)S(1)}, s32[]{:S(2)}) async-start(s8[18874368]{0:T(1024)(128)(4,1)} %bitcast.295), calls=%async_computation.25 | async-start | bytes 8388608
  359.9 12.5 %collective-permute-start.4 = (bf16[64,3072]{1,0:T(8,128)(2,1)}, bf16[64,3072]{1,0:T(8,128)(2,1)}, u32[]{:S(2)}, u32[]{:S(2)}) collective-permute-start(bf16[64,3072]{1,0:T(8,128)(2,1)} %get-tuple-element.6), channel_id=1, source_target_pairs={{0,32},{32,64},{64,96},{1,33},{33,65},{65,97},{2,34},{34,66},{66,9... | collective-permute-start | bytes 1179656 | tf_op jit(solution)/shard_map/ppermute | solution.py:12
  377.3 15.6 %slice-start.25 = ((s8[18874368]{0:T(1024)(128)(4,1)}), s8[4194304]{0:T(1024)(128)(4,1)S(1)}, s32[]{:S(2)}) async-start(s8[18874368]{0:T(1024)(128)(4,1)} %bitcast.297), calls=%async_computation.27 | async-start | bytes 8388608
  377.3 15.6 %slice-start.26 = ((s8[18874368]{0:T(1024)(128)(4,1)}), s8[4194304]{0:T(1024)(128)(4,1)S(1)}, s32[]{:S(2)}) async-start(s8[18874368]{0:T(1024)(128)(4,1)} %bitcast.297), calls=%async_computation.28 | async-start | bytes 8388608
  377.3 15.6 %slice-start.27 = ((s8[18874368]{0:T(1024)(128)(4,1)}), s8[4194304]{0:T(1024)(128)(4,1)S(1)}, s32[]{:S(2)}) async-start(s8[18874368]{0:T(1024)(128)(4,1)} %bitcast.297), calls=%async_computation.29 | async-start | bytes 8388608
  377.3 15.6 %slice-start.28 = ((s8[18874368]{0:T(1024)(128)(4,1)}), s8[4194304]{0:T(1024)(128)(4,1)S(1)}, s32[]{:S(2)}) async-start(s8[18874368]{0:T(1024)(128)(4,1)} %bitcast.297), calls=%async_computation.30 | async-start | bytes 8388608
  (19 other events, 106.9 us)
Sparse Core Ops, SparseCore 0:
  9.5 56.4 all-gather.7
  68.1 121.7 all-gather.5
where the time goes:
time: 412 us; the launch traced here: 404 us
  waiting for transfers between devices  180 us (44%)
  matrix products  96.2 us (23%)
  between operations  33.4 us (8%)
  blocking collectives  32.9 us (8%)
  local copies, waits for them, and re-layouts  28.2 us (7%)
  other arithmetic  18 us (4%)
  starting transfers between devices  15.4 us (4%)
    all_gather x1, waiting for transfers between devices, body(): w_whole = lax.all_gather(w_local, 'seq', axis=0, tiled=True)  107 us
    dot_general x6, matrix products, body(): query = jnp.dot(normed, w_whole, preferred_element_type=jnp.float32)  60 us
    ppermute x5, waiting for transfers between devices, passed_along(): return lax.ppermute(block, axis, route)  36.8 us
    all_gather x1, waiting for transfers between devices, body(): kv_whole = lax.all_gather(kv_local, 'seq', axis=0, tiled=True)  35.1 us
    dot_general x6, matrix products, body(): jnp.dot(lax.all_gather(attended, 'mp', axis=1, tiled=True), out_weight, p...  25.6 us
    all_gather x6, blocking collectives, body(): whole = lax.all_gather(current, 'mp', axis=1, tiled=True)  20 us
    ppermute x5, starting transfers between devices, passed_along(): return lax.ppermute(block, axis, route)  15.4 us
    all_gather x6, blocking collectives, body(): lax.all_gather(attended, 'mp', axis=1, tiled=True)  13 us
  transfers between devices with their start and end apart: 7, of which 7 were waited for; matrix products, arithmetic and copies ran while one was open for 7% of the time, Pallas kernels for 0%

commit v1 on v0

v1 whole, which is shorter than its diff:
```python
import functools

import jax
import jax.numpy as jnp
from jax import lax
from jax.experimental import pallas as pl
from jax.experimental.pallas import tpu as pltpu
from jax.sharding import PartitionSpec as P

HEAD_DIM = 128
TILE = 256
LONGEST = 400
MIB = 1024 * 1024

SMEM = pl.BlockSpec(memory_space=pltpu.SMEM)
VMEM = pl.BlockSpec(memory_space=pltpu.VMEM)
HBM = pl.BlockSpec(memory_space=pltpu.HBM)


def attend_tile(n, query, valid, keys, values, out_ref):
    heads = range(TILE // HEAD_DIM)
    cols = [slice(n * TILE + h * HEAD_DIM, n * TILE + (h + 1) * HEAD_DIM) for h in heads]
    scores = [
        lax.dot_general(
            query[:, h * HEAD_DIM : (h + 1) * HEAD_DIM],
            keys[:, cols[h]],
            (((1,), (1,)), ((), ())),
            preferred_element_type=jnp.float32,
        )
        * HEAD_DIM ** (-0.5)
        for h in heads
    ]
    scores = [jnp.where(valid, s, -1e30) for s in scores]
    tops = [jnp.max(s, axis=-1, keepdims=True) for s in scores]
    weights = [jnp.where(valid, jnp.exp(s - t), 0.0) for s, t in zip(scores, tops)]
    totals = [jnp.sum(w, axis=-1, keepdims=True) for w in weights]
    sums = [
        jnp.dot(w.astype(jnp.bfloat16), values[:, c], preferred_element_type=jnp.float32)
        for w, c in zip(weights, cols)
    ]
    for c, acc, total in zip(cols, sums, totals):
        out_ref[:, c] = (acc / total).astype(jnp.bfloat16)


def keep_kernel(whole_ref, kept_ref, sems):
    count, blocks, depth, tile = kept_ref.shape
    copies = [
        pltpu.make_async_copy(
            whole_ref.at[:, pl.ds(0, depth), pl.ds(n * tile, tile)], kept_ref.at[n], sems.at[n]
        )
        for n in range(count)
    ]
    for copy in copies:
        copy.start()
    for copy in copies:
        copy.wait()


def keep(whole, depth):
    return pl.pallas_call(
        keep_kernel,
        out_shape=jax.ShapeDtypeStruct((whole.shape[2] // TILE, whole.shape[0], depth, TILE), jnp.bfloat16),
        in_specs=[HBM],
        out_specs=VMEM,
        scratch_shapes=[pltpu.SemaphoreType.DMA((whole.shape[2] // TILE,))],
        compiler_params=pltpu.CompilerParams(vmem_limit_bytes=22 * MIB),
    )(whole)


def attend_kernel(
    lengths, order, slot, x_ref, kept_ref, whole_ref, out_ref, keys, values, kv_sems
):
    tokens, features = x_ref.shape
    tiles, blocks, depth, _ = kept_ref.shape
    rows = keys.shape[1]

    sample = order[slot[0]]
    start = jnp.int32(0)
    for i in range(lengths.shape[0] - 1):
        start = start + jnp.where(i < sample, lengths[i], 0)
    stop = start + lengths[sample]
    first = jnp.minimum(start // rows, blocks - keys.shape[0])
    captions = [
        pltpu.make_async_copy(
            whole_ref.at[pl.ds(first, keys.shape[0]), pl.ds(depth + i * rows, rows)],
            buffer,
            kv_sems.at[i],
        )
        for i, buffer in enumerate((keys, values))
    ]
    for copy in captions:
        copy.start()
    span = keys.shape[0] * rows
    row = first * rows + lax.broadcasted_iota(jnp.int32, (1, span), 1)
    valid = (row >= start) & (row < stop)
    keys_2d = keys.reshape(span, keys.shape[2])
    values_2d = values.reshape(span, values.shape[2])
    chunk = 512
    squares = jnp.zeros((tokens, chunk), jnp.float32)
    for at in range(0, features, chunk):
        xf = x_ref[:, at : at + chunk].astype(jnp.float32)
        squares = squares + xf * xf
    scale = lax.rsqrt(jnp.sum(squares, axis=-1, keepdims=True) / features + 1e-06)
    query = None
    for n in range(tiles):
        if n == 1:
            for copy in captions:
                copy.wait()
        weight = kept_ref[n].reshape(blocks * depth, TILE)
        product = jnp.dot(x_ref[...], weight, preferred_element_type=jnp.float32)
        if n > 0:
            attend_tile(n - 1, query, valid, keys_2d, values_2d, out_ref)
        query = (product * scale).astype(jnp.bfloat16)
    attend_tile(tiles - 1, query, valid, keys_2d, values_2d, out_ref)


def attend(lengths, order, slot, x, kept, whole):
    tokens, features = x.shape
    blocks, block, width = whole.shape
    depth = features // blocks
    rows = (block - depth) // 2
    span = min((LONGEST + rows - 2) // rows + 1, blocks)
    caption = pltpu.VMEM((span, rows, width), jnp.bfloat16)
    return pl.pallas_call(
        attend_kernel,
        out_shape=jax.ShapeDtypeStruct((tokens, width), jnp.bfloat16),
        in_specs=[SMEM] * 3 + [VMEM, VMEM, HBM],
        out_specs=VMEM,
        scratch_shapes=[
            caption,
            caption,
            pltpu.SemaphoreType.DMA((2,)),
        ],
        compiler_params=pltpu.CompilerParams(vmem_limit_bytes=ATTEND_MIB * MIB),
        cost_estimate=pl.CostEstimate(
            flops=2 * tokens * features * width,
            bytes_accessed=2 * features * width,
            transcendentals=0,
        ),
    )(lengths, order, slot, x, kept, whole)


ATTEND_MIB = 14


def project_kernel(column, a_ref, w_ref, x_ref, out_ref):
    tile = 512

    @pl.loop(0, out_ref.shape[1] // tile)
    def _(n):
        cols = pl.ds(pl.multiple_of(n * tile, tile), tile)
        from_cols = pl.ds(pl.multiple_of(column + n * tile, tile), tile)
        p = jnp.dot(a_ref[...], w_ref[:, from_cols], preferred_element_type=jnp.float32)
        out_ref[:, cols] = (x_ref[:, cols].astype(jnp.float32) + p).astype(jnp.bfloat16)


def project(attended, w, x, column):
    return pl.pallas_call(
        functools.partial(project_kernel, column),
        out_shape=jax.ShapeDtypeStruct(x.shape, jnp.bfloat16),
        in_specs=[VMEM] * 3,
        out_specs=VMEM,
        compiler_params=pltpu.CompilerParams(vmem_limit_bytes=22 * MIB),
        cost_estimate=pl.CostEstimate(
            flops=2 * x.shape[0] * w.shape[0] * x.shape[1],
            bytes_accessed=2 * w.shape[0] * x.shape[1],
            transcendentals=0,
        ),
    )(attended, w, x)


def body(video, caption_kv, caption_lengths, order, gains, w_query, w_out):
    samples = video.shape[0]
    segments = lax.axis_size("segment")
    here = lax.axis_index("segment")
    seq = lax.axis_index("seq")
    depth = w_query.shape[1]

    gain = lax.dynamic_slice_in_dim(gains[0], seq * depth, depth)
    weight = (w_query[0].astype(jnp.float32) * gain[:, None]).astype(jnp.bfloat16)
    local = jnp.concatenate(
        [weight, caption_kv[0, :, 0, :], caption_kv[0, :, 1, :]], axis=0
    )
    gathered = lax.all_gather(local, "seq", axis=0)
    kept = keep(gathered, depth)

    out_weight = w_out[0]
    received = None
    results = []
    last = samples + segments - 2
    for tick in range(last + 1):
        slot = jnp.clip(tick - here, 0, samples - 1).astype(jnp.int32)[None]
        if tick < samples:
            current = lax.dynamic_index_in_dim(video, order[tick], 0, keepdims=False)
            if tick:
                current = jnp.where(here == 0, current, received)
        else:
            current = received
        whole = lax.all_gather(current, "mp", axis=1, tiled=True)
        attended = attend(caption_lengths, order, slot, whole, kept, gathered)
        attended = lax.all_gather(attended, "mp", axis=1, tiled=True)
        mixed = project(attended, out_weight, current, 0)
        if tick < last:
            received = lax.ppermute(
                mixed, "segment", [(i, i + 1) for i in range(segments - 1)]
            )
        results.append(mixed)
    stacked = jnp.stack(results)
    return lax.dynamic_slice_in_dim(stacked, here, samples, 0)[None]


def solution(mesh):
    in_specs = (
        P(None, "seq", "mp"),
        P("segment", "seq", None, "mp"),
        P(),
        P(),
        P("segment", None),
        P("segment", "seq", "mp"),
        P("segment", None, "mp"),
    )
    out_specs = P("segment", None, "seq", "mp")
    return jax.shard_map(body, mesh=mesh, in_specs=in_specs, out_specs=out_specs, check_vma=False)
```

time: 412 us -> 331 us (0.80); the launches traced: 404 us -> 330 us
  matrix products: 96.2 us -> 0 us
  Pallas kernels: 0 us -> 69.1 us
  local copies, waits for them, and re-layouts: 28.2 us -> 3.75 us
  between operations: 33.4 us -> 19.2 us
  other arithmetic: 18 us -> 5.71 us
  waiting for transfers between devices: 180 us -> 185 us
    dot_general x24 -> x0, matrix products: 96.2 us -> none  [the longest x6 60 us: body(): query = jnp.dot(normed, w_whole, preferred_element_type=jnp.float32)]
    pallas_call x0 -> x12, Pallas kernels: none -> 69.1 us  [the longest x6 42.3 us: attend(): pl.pallas_call(attend_kernel, out_shape=jax.ShapeDtypeStruct((tokens, wid...]
    all_gather x1 -> x0, local copies, waits for them, and re-layouts: 12.5 us -> none  [body(): kv_whole = lax.all_gather(kv_local, 'seq', axis=0, tiled=True)]
    ppermute x5, waiting for transfers between devices: 36.8 us -> 45.4 us  [body(): lax.ppermute(mixed, 'segment', [(i, i + 1) for i in range(segments - 1)])]
    unnamed x89 -> x27, local copies, waits for them, and re-layouts: 7.61 us -> 0.19 us
    select_n x6 -> x2, other arithmetic: 6.82 us -> 0.11 us  [body(): current = jnp.where(here == 0, current, received)]
    reduce_sum x12 -> x0, other arithmetic: 5.79 us -> none  [the longest x6 4.29 us: block_terms(): total = jnp.sum(weights, axis=-1)]
    all_gather x2 -> x1, waiting for transfers between devices: 142 us -> 140 us  [body(): gathered = lax.all_gather(local, 'seq', axis=0)]
  transfers between devices with their start and end apart: 7 -> 6, of which waited for: 7 -> 6; matrix products, arithmetic and copies ran while one was open for 7% -> 0% of each run, Pallas kernels for 0% -> 0%
where the time goes in v1:
time: 331 us; the launch traced here: 330 us
  waiting for transfers between devices  185 us (56%)
  Pallas kernels  69.1 us (21%)
  blocking collectives  31.9 us (10%)
  between operations  19.2 us (6%)
  starting transfers between devices  15.5 us (5%)
  other arithmetic  5.71 us (2%)
  local copies, waits for them, and re-layouts  3.75 us (1%)
    all_gather x1, waiting for transfers between devices, body(): gathered = lax.all_gather(local, 'seq', axis=0)  140 us
    ppermute x5, waiting for transfers between devices, body(): lax.ppermute(mixed, 'segment', [(i, i + 1) for i in range(segments - 1)])  45.4 us
    pallas_call x6, Pallas kernels, attend(): pl.pallas_call(attend_kernel, out_shape=jax.ShapeDtypeStruct((tokens, wid...  42.3 us
    pallas_call x5, Pallas kernels, project(): pl.pallas_call(functools.partial(project_kernel, column), out_shape=jax.S...  20.2 us
    all_gather x6, blocking collectives, body(): whole = lax.all_gather(current, 'mp', axis=1, tiled=True)  19 us
    ppermute x5, starting transfers between devices, body(): lax.ppermute(mixed, 'segment', [(i, i + 1) for i in range(segments - 1)])  15.5 us
    all_gather x6, blocking collectives, body(): attended = lax.all_gather(attended, 'mp', axis=1, tiled=True)  12.8 us
  transfers between devices with their start and end apart: 6, of which 6 were waited for; matrix products, arithmetic and copies ran while one was open for 0% of the time, Pallas kernels for 0%

profile of v1, /device:TPU:3, one launch (start us, length us, event | category | flops | bytes accessed | tf_op | source)
XLA Modules:
  0.0 330.5 jit_solution(128009706325324461)
XLA Ops:
  16.1 2.7 all-gather
  18.8 139.9 %all-gather.4.cloned.1.call-done = bf16[7680,1536]{1,0:T(8,128)(2,1)} async-done(((bf16[480,1536]{1,0:T(8,128)(2,1)}), bf16[7680,1536]{1,0:T(8,128)(2,1)}) %all-gather.4.cloned.1.call-update) | async-done | bytes 23592976 | tf_op jit(solution)/shard_map/all_gather | solution.py:184
  158.7 6.6 %shard_map.73.kept_ref = bf16[6,16,384,256]{3,2,1,0:T(8,128)(2,1)S(1)} custom-call(bf16[16,480,1536]{2,1,0:T(8,128)(2,1)} %bitcast.48), custom_call_target="tpu_custom_call" | custom-call | tf_op jit(solution)/shard_map/pallas_call | solution.py:60
  165.4 7.3 %shard_map.74 = bf16[64,1536]{1,0:T(8,128)(2,1)S(1)} custom-call(s32[3]{0:T(128)S(1)} %copy-done.3, s32[3]{0:T(128)S(1)} %copy-done.2, s32[1]{0:T(128)} %bitcast.slot, bf16[64,6144]{1,0:T(8,128)(2,1)S(1)} %bitcast.47, bf16[6,16,384,256]{3,2,1,0:T(8,128)(2,1)S(1)} %shard_map.73.kept_ref, bf16[16,480,1536]{2,1,0:T(8,128)(2,1)} %bitcast.49), custom_call_target="tpu_custom_call" | custom-call | flops 1207959552 | bytes 18874368 | tf_op jit(solution)/shard_map/pallas_call | solution.py:124
  172.7 2.4 all_gather.45.a_ref
  175.1 4.0 %shard_map.75 = bf16[64,3072]{1,0:T(8,128)(2,1)S(1)} custom-call(bf16[64,3072]{1,0:T(8,128)(2,1)S(1)} %all_gather.45.a_ref, bf16[3072,3072]{1,0:T(8,128)(2,1)S(1)} %bitcast.41, bf16[64,3072]{1,0:T(8,128)(2,1)S(1)} %fusion.3.x_ref), custom_call_target="tpu_custom_call" | custom-call | flops 1207959552 | bytes 18874368 | tf_op jit(solution)/shard_map/pallas_call | solution.py:158
  179.2 3.1 collective-permute-start
  182.3 9.1 %collective-permute-done = bf16[64,3072]{1,0:T(8,128)(2,1)S(1)} collective-permute-done((bf16[64,3072]{1,0:T(8,128)(2,1)S(1)}, bf16[64,3072]{1,0:T(8,128)(2,1)S(1)}, u32[]{:S(2)}, u32[]{:S(2)}) %collective-permute-start) | collective-permute-done | bytes 393248 | tf_op jit(solution)/shard_map/ppermute | solution.py:204
  191.4 3.2 all_gather.46.x_ref
  194.6 7.0 %shard_map.76 = bf16[64,1536]{1,0:T(8,128)(2,1)S(1)} custom-call(s32[3]{0:T(128)S(1)} %copy-done.3, s32[3]{0:T(128)S(1)} %copy-done.2, s32[1]{0:T(128)} %bitcast.10.slot, bf16[64,6144]{1,0:T(8,128)(2,1)S(1)} %all_gather.46.x_ref, bf16[6,16,384,256]{3,2,1,0:T(8,128)(2,1)S(1)} %shard_map.73.kept_ref, bf16[16,480,1536]{2,1,0:T(8,128)(2,1)} %bitcast.50), custom_call_target="tpu_custom_call" | custom-call | flops 1207959552 | bytes 18874368 | tf_op jit(solution)/shard_map/pallas_call | solution.py:124
  203.7 4.0 %shard_map.77 = bf16[64,3072]{1,0:T(8,128)(2,1)S(1)} custom-call(bf16[64,3072]{1,0:T(8,128)(2,1)S(1)} %all_gather.47.a_ref, bf16[3072,3072]{1,0:T(8,128)(2,1)S(1)} %bitcast.42, bf16[64,3072]{1,0:T(8,128)(2,1)S(1)} %bitcast_select_fusion.1.x_ref), custom_call_target="tpu_custom_call" | custom-call | flops 1207959552 | bytes 18874368 | tf_op jit(solution)/shard_map/pallas_call | solution.py:158
  207.8 3.1 collective-permute-start.1
  210.9 9.1 %collective-permute-done.1 = bf16[64,3072]{1,0:T(8,128)(2,1)S(1)} collective-permute-done((bf16[64,3072]{1,0:T(8,128)(2,1)S(1)}, bf16[64,3072]{1,0:T(8,128)(2,1)S(1)}, u32[]{:S(2)}, u32[]{:S(2)}) %collective-permute-start.1) | collective-permute-done | bytes 393248 | tf_op jit(solution)/shard_map/ppermute | solution.py:204
  220.1 3.4 %all_gather.48.x_ref = bf16[64,6144]{1,0:T(8,128)(2,1)S(1)} all-gather(bf16[64,3072]{1,0:T(8,128)(2,1)S(1)} %bitcast_select_fusion.x_ref), channel_id=1, replica_groups=mesh['segment'=4,'seq'=16,'mp'=2] {'mp'}, dimensions={1}, use_global_device_ids=true | all-gather | bytes 1179648 | tf_op jit(solution)/shard_map/all_gather | solution.py:199
  223.5 7.0 %shard_map.78 = bf16[64,1536]{1,0:T(8,128)(2,1)S(1)} custom-call(s32[3]{0:T(128)S(1)} %copy-done.3, s32[3]{0:T(128)S(1)} %copy-done.2, s32[1]{0:T(128)} %bitcast.14.slot, bf16[64,6144]{1,0:T(8,128)(2,1)S(1)} %all_gather.48.x_ref, bf16[6,16,384,256]{3,2,1,0:T(8,128)(2,1)S(1)} %shard_map.73.kept_ref, bf16[16,480,1536]{2,1,0:T(8,128)(2,1)} %bitcast.51), custom_call_target="tpu_custom_call" | custom-call | flops 1207959552 | bytes 18874368 | tf_op jit(solution)/shard_map/pallas_call | solution.py:124
  232.6 4.0 %shard_map.79 = bf16[64,3072]{1,0:T(8,128)(2,1)S(1)} custom-call(bf16[64,3072]{1,0:T(8,128)(2,1)S(1)} %all_gather.49.a_ref, bf16[3072,3072]{1,0:T(8,128)(2,1)S(1)} %bitcast.43, bf16[64,3072]{1,0:T(8,128)(2,1)S(1)} %bitcast_select_fusion.x_ref), custom_call_target="tpu_custom_call" | custom-call | flops 1207959552 | bytes 18874368 | tf_op jit(solution)/shard_map/pallas_call | solution.py:158
  236.6 3.1 collective-permute-start.2
  239.7 9.1 %collective-permute-done.2.x_ref = bf16[64,3072]{1,0:T(8,128)(2,1)S(1)} collective-permute-done((bf16[64,3072]{1,0:T(8,128)(2,1)S(1)}, bf16[64,3072]{1,0:T(8,128)(2,1)S(1)}, u32[]{:S(2)}, u32[]{:S(2)}) %collective-permute-start.2) | collective-permute-done | bytes 393248 | tf_op jit(solution)/shard_map/ppermute | solution.py:204
  248.8 3.2 all_gather.50.x_ref
  252.0 7.0 %shard_map.80 = bf16[64,1536]{1,0:T(8,128)(2,1)S(1)} custom-call(s32[3]{0:T(128)S(1)} %copy-done.3, s32[3]{0:T(128)S(1)} %copy-done.2, s32[1]{0:T(128)} %bitcast.18.slot, bf16[64,6144]{1,0:T(8,128)(2,1)S(1)} %all_gather.50.x_ref, bf16[6,16,384,256]{3,2,1,0:T(8,128)(2,1)S(1)} %shard_map.73.kept_ref, bf16[16,480,1536]{2,1,0:T(8,128)(2,1)} %bitcast.52), custom_call_target="tpu_custom_call" | custom-call | flops 1207959552 | bytes 18874368 | tf_op jit(solution)/shard_map/pallas_call | solution.py:124
  261.1 4.0 %shard_map.81 = bf16[64,3072]{1,0:T(8,128)(2,1)S(1)} custom-call(bf16[64,3072]{1,0:T(8,128)(2,1)S(1)} %all_gather.51.a_ref, bf16[3072,3072]{1,0:T(8,128)(2,1)S(1)} %bitcast.44, bf16[64,3072]{1,0:T(8,128)(2,1)S(1)} %collective-permute-done.2.x_ref), custom_call_target="tpu_custom_call" | custom-call | flops 1207959552 | bytes 18874368 | tf_op jit(solution)/shard_map/pallas_call | solution.py:158
  265.1 3.1 collective-permute-start.3
  268.3 9.1 %collective-permute-done.3.x_ref = bf16[64,3072]{1,0:T(8,128)(2,1)S(1)} collective-permute-done((bf16[64,3072]{1,0:T(8,128)(2,1)S(1)}, bf16[64,3072]{1,0:T(8,128)(2,1)S(1)}, u32[]{:S(2)}, u32[]{:S(2)}) %collective-permute-start.3) | collective-permute-done | bytes 393248 | tf_op jit(solution)/shard_map/ppermute | solution.py:204
  277.3 3.4 %all_gather.52.x_ref = bf16[64,6144]{1,0:T(8,128)(2,1)S(1)} all-gather(bf16[64,3072]{1,0:T(8,128)(2,1)S(1)} %collective-permute-done.3.x_ref), channel_id=1, replica_groups=mesh['segment'=4,'seq'=16,'mp'=2] {'mp'}, dimensions={1}, use_global_device_ids=true | all-gather | bytes 1179648 | tf_op jit(solution)/shard_map/all_gather | solution.py:199
  280.8 7.0 %shard_map.82 = bf16[64,1536]{1,0:T(8,128)(2,1)S(1)} custom-call(s32[3]{0:T(128)S(1)} %copy-done.3, s32[3]{0:T(128)S(1)} %copy-done.2, s32[1]{0:T(128)} %bitcast.20.slot, bf16[64,6144]{1,0:T(8,128)(2,1)S(1)} %all_gather.52.x_ref, bf16[6,16,384,256]{3,2,1,0:T(8,128)(2,1)S(1)} %shard_map.73.kept_ref, bf16[16,480,1536]{2,1,0:T(8,128)(2,1)} %bitcast.53), custom_call_target="tpu_custom_call" | custom-call | flops 1207959552 | bytes 18874368 | tf_op jit(solution)/shard_map/pallas_call | solution.py:124
  289.9 4.0 %shard_map.83 = bf16[64,3072]{1,0:T(8,128)(2,1)S(1)} custom-call(bf16[64,3072]{1,0:T(8,128)(2,1)S(1)} %all_gather.53.a_ref, bf16[3072,3072]{1,0:T(8,128)(2,1)S(1)} %bitcast.45, bf16[64,3072]{1,0:T(8,128)(2,1)S(1)} %collective-permute-done.3.x_ref), custom_call_target="tpu_custom_call" | custom-call | flops 1207959552 | bytes 18874368 | tf_op jit(solution)/shard_map/pallas_call | solution.py:158
  293.9 3.1 collective-permute-start.4
  297.0 9.1 %collective-permute-done.4 = bf16[64,3072]{1,0:T(8,128)(2,1)S(1)} collective-permute-done((bf16[64,3072]{1,0:T(8,128)(2,1)S(1)}, bf16[64,3072]{1,0:T(8,128)(2,1)S(1)}, u32[]{:S(2)}, u32[]{:S(2)}) %collective-permute-start.4) | collective-permute-done | bytes 393248 | tf_op jit(solution)/shard_map/ppermute | solution.py:204
  306.1 3.2 all_gather.54.x_ref
  309.3 7.0 %shard_map.84 = bf16[64,1536]{1,0:T(8,128)(2,1)S(1)} custom-call(s32[3]{0:T(128)S(1)} %copy-done.3, s32[3]{0:T(128)S(1)} %copy-done.2, s32[1]{0:T(128)} %bitcast.22.slot, bf16[64,6144]{1,0:T(8,128)(2,1)S(1)} %all_gather.54.x_ref, bf16[6,16,384,256]{3,2,1,0:T(8,128)(2,1)S(1)} %shard_map.73.kept_ref, bf16[16,480,1536]{2,1,0:T(8,128)(2,1)} %bitcast.54), custom_call_target="tpu_custom_call" | custom-call | flops 1207959552 | bytes 18874368 | tf_op jit(solution)/shard_map/pallas_call | solution.py:124
  316.3 2.1 all_gather.55
  318.4 4.1 %shard_map.85 = bf16[6,64,3072]{2,1,0:T(8,128)(2,1)S(1)} fusion(bf16[6,64,3072]{2,1,0:T(8,128)(2,1)S(1)} %bitcast_dynamic-update-slice_fusion.1, bf16[64,3072]{1,0:T(8,128)(2,1)S(1)} %all_gather.55, bf16[3072,3072]{1,0:T(8,128)(2,1)S(1)} %bitcast.46, bf16[64,3072]{1,0:T(8,128)(2,1)S(1)} %collective-permute-done.4), kind=kCustom, calls=%fused_computation.4 | custom fusion | flops 1207959552 | bytes 20054016 | tf_op jit(solution)/shard_map/pallas_call | solution.py:158
  (45 shorter events, 13.8 us)
Async XLA Ops:
  6.5 1.7 copy-start
  6.5 1.8 copy-start.5
  6.5 152.1 %all-gather.4.cloned.1.call-start = ((), (), s32[]{:S(2)}) async-start(), calls=%async_computation | async-start | bytes 25067520 | tf_op jit(solution)/shard_map/all_gather | solution.py:184
  8.6 1.3 copy-start.2
  8.6 7.4 %copy-start.4 = (bf16[3,64,3072]{2,1,0:T(8,128)(2,1)S(1)}, bf16[3,64,3072]{2,1,0:T(8,128)(2,1)}, u32[]{:S(2)}) copy-start(bf16[3,64,3072]{2,1,0:T(8,128)(2,1)} %param.7) | copy-start | bytes 3538948
  158.7 6.6 %copy-start.3 = (s32[3]{0:T(128)S(1)}, s32[3]{0:T(128)}, u32[]{:S(2)}) copy-start(s32[3]{0:T(128)} %lengths.11) | copy-start | bytes 40
  165.3 9.8 %slice-start = ((s8[18874368]{0:T(1024)(128)(4,1)}), s8[4194304]{0:T(1024)(128)(4,1)S(1)}, s32[]{:S(2)}) async-start(s8[18874368]{0:T(1024)(128)(4,1)} %bitcast.39), calls=%async_computation.1 | async-start | bytes 8388608
  165.3 9.8 %slice-start.1 = ((s8[18874368]{0:T(1024)(128)(4,1)}), s8[4194304]{0:T(1024)(128)(4,1)S(1)}, s32[]{:S(2)}) async-start(s8[18874368]{0:T(1024)(128)(4,1)} %bitcast.39), calls=%async_computation.2 | async-start | bytes 8388608
  165.3 9.8 %slice-start.2 = ((s8[18874368]{0:T(1024)(128)(4,1)}), s8[4194304]{0:T(1024)(128)(4,1)S(1)}, s32[]{:S(2)}) async-start(s8[18874368]{0:T(1024)(128)(4,1)} %bitcast.39), calls=%async_computation.3 | async-start | bytes 8388608
  165.4 9.7 %slice-start.3 = ((s8[18874368]{0:T(1024)(128)(4,1)}), s8[4194304]{0:T(1024)(128)(4,1)S(1)}, s32[]{:S(2)}) async-start(s8[18874368]{0:T(1024)(128)(4,1)} %bitcast.39), calls=%async_computation.4 | async-start | bytes 8388608
  165.4 9.7 %slice-start.4 = ((s8[18874368]{0:T(1024)(128)(4,1)}), s8[2097152]{0:T(1024)(128)(4,1)S(1)}, s32[]{:S(2)}) async-start(s8[18874368]{0:T(1024)(128)(4,1)} %bitcast.39), calls=%async_computation.5 | async-start | bytes 4194304
  179.2 12.2 %collective-permute-start = (bf16[64,3072]{1,0:T(8,128)(2,1)S(1)}, bf16[64,3072]{1,0:T(8,128)(2,1)S(1)}, u32[]{:S(2)}, u32[]{:S(2)}) collective-permute-start(bf16[64,3072]{1,0:T(8,128)(2,1)S(1)} %shard_map.75), channel_id=1, source_target_pairs={{0,32},{32,64},{64,96},{1,33},{33,65},{65,97},{2,34},{34,66},{66,9... | collective-permute-start | bytes 1179656 | tf_op jit(solution)/shard_map/ppermute | solution.py:204
  207.8 12.2 %collective-permute-start.1 = (bf16[64,3072]{1,0:T(8,128)(2,1)S(1)}, bf16[64,3072]{1,0:T(8,128)(2,1)S(1)}, u32[]{:S(2)}, u32[]{:S(2)}) collective-permute-start(bf16[64,3072]{1,0:T(8,128)(2,1)S(1)} %shard_map.77), channel_id=1, source_target_pairs={{0,32},{32,64},{64,96},{1,33},{33,65},{65,97},{2,34},{34,66},{66,9... | collective-permute-start | bytes 1179656 | tf_op jit(solution)/shard_map/ppermute | solution.py:204
  236.6 12.2 %collective-permute-start.2 = (bf16[64,3072]{1,0:T(8,128)(2,1)S(1)}, bf16[64,3072]{1,0:T(8,128)(2,1)S(1)}, u32[]{:S(2)}, u32[]{:S(2)}) collective-permute-start(bf16[64,3072]{1,0:T(8,128)(2,1)S(1)} %shard_map.79), channel_id=1, source_target_pairs={{0,32},{32,64},{64,96},{1,33},{33,65},{65,97},{2,34},{34,66},{66,9... | collective-permute-start | bytes 1179656 | tf_op jit(solution)/shard_map/ppermute | solution.py:204
  265.1 12.2 %collective-permute-start.3 = (bf16[64,3072]{1,0:T(8,128)(2,1)S(1)}, bf16[64,3072]{1,0:T(8,128)(2,1)S(1)}, u32[]{:S(2)}, u32[]{:S(2)}) collective-permute-start(bf16[64,3072]{1,0:T(8,128)(2,1)S(1)} %shard_map.81), channel_id=1, source_target_pairs={{0,32},{32,64},{64,96},{1,33},{33,65},{65,97},{2,34},{34,66},{66,9... | collective-permute-start | bytes 1179656 | tf_op jit(solution)/shard_map/ppermute | solution.py:204
  293.9 12.2 %collective-permute-start.4 = (bf16[64,3072]{1,0:T(8,128)(2,1)S(1)}, bf16[64,3072]{1,0:T(8,128)(2,1)S(1)}, u32[]{:S(2)}, u32[]{:S(2)}) collective-permute-start(bf16[64,3072]{1,0:T(8,128)(2,1)S(1)} %shard_map.83), channel_id=1, source_target_pairs={{0,32},{32,64},{64,96},{1,33},{33,65},{65,97},{2,34},{34,66},{66,9... | collective-permute-start | bytes 1179656 | tf_op jit(solution)/shard_map/ppermute | solution.py:204
  318.4 5.2 %copy-start.1 = (f32[1,6144]{1,0:T(1,128)S(1)}, f32[1,6144]{1,0:T(1,128)}, u32[]{:S(2)}) copy-start(f32[1,6144]{1,0:T(1,128)} %param.11) | copy-start | bytes 73732
Sparse Core Ops, SparseCore 0:
  10.0 148.6 all-gather.3

commit v2 on v1

v2 whole, which is shorter than its diff:
```python
import functools

import jax
import jax.numpy as jnp
from jax import lax
from jax.experimental import pallas as pl
from jax.experimental.pallas import tpu as pltpu
from jax.sharding import PartitionSpec as P

HEAD_DIM = 128
TILE = 256
WINDOW = 416
SIDE = 4
MIB = 1024 * 1024

SMEM = pl.BlockSpec(memory_space=pltpu.SMEM)
VMEM = pl.BlockSpec(memory_space=pltpu.VMEM)
HBM = pl.BlockSpec(memory_space=pltpu.HBM)


def attend_tile(n, query, valid, base, k_ref, v_ref, out_ref):
    heads = range(TILE // HEAD_DIM)
    cols = [slice(n * TILE + h * HEAD_DIM, n * TILE + (h + 1) * HEAD_DIM) for h in heads]
    scores = [
        lax.dot_general(
            query[:, h * HEAD_DIM : (h + 1) * HEAD_DIM],
            k_ref[pl.ds(base, WINDOW), cols[h]],
            (((1,), (1,)), ((), ())),
            preferred_element_type=jnp.float32,
        )
        * HEAD_DIM ** (-0.5)
        for h in heads
    ]
    scores = [jnp.where(valid, s, -1e30) for s in scores]
    tops = [jnp.max(s, axis=-1, keepdims=True) for s in scores]
    weights = [jnp.where(valid, jnp.exp(s - t), 0.0) for s, t in zip(scores, tops)]
    totals = [jnp.sum(w, axis=-1, keepdims=True) for w in weights]
    sums = [
        jnp.dot(
            w.astype(jnp.bfloat16),
            v_ref[pl.ds(base, WINDOW), c],
            preferred_element_type=jnp.float32,
        )
        for w, c in zip(weights, cols)
    ]
    for c, acc, total in zip(cols, sums, totals):
        out_ref[:, c] = (acc / total).astype(jnp.bfloat16)


def shift(block, axis, step):
    dz, dy = (step, 0) if axis == "z" else (0, step)
    pairs = [
        (z * SIDE + y, (z + dz) % SIDE * SIDE + (y + dy) % SIDE)
        for z in range(SIDE)
        for y in range(SIDE)
    ]
    return lax.ppermute(block, "seq", pairs)


def ring(block, axis):
    half = block.shape[0] // 2
    below = shift(block, axis, 1)
    above = shift(block, axis, -1)
    return below, above, shift(below[:half], axis, 1), shift(above[half:], axis, -1)


def pack_kernel(axes, place, *refs):
    count = len(axes)
    ins, outs, sems = refs[: 5 * count], refs[5 * count : 6 * count], refs[-1]
    copies = []
    for group, (axis, slab) in enumerate(zip(axes, outs)):
        at = place[0 if axis == "z" else 1]
        own, below, above, low, high = ins[5 * group : 5 * group + 5]
        half = own.shape[0] // 2
        for src, dst in (
            (own, slab.at[at]),
            (below, slab.at[(at + 3) % SIDE]),
            (above, slab.at[(at + 1) % SIDE]),
            (low, slab.at[(at + 2) % SIDE, pl.ds(0, half)]),
            (high, slab.at[(at + 2) % SIDE, pl.ds(half, half)]),
        ):
            copies.append(pltpu.make_async_copy(src, dst, sems.at[len(copies)]))
    for copy in copies:
        copy.start()
    for copy in copies:
        copy.wait()


def pack(place, axes, rings):
    shape = jax.ShapeDtypeStruct((SIDE,) + rings[0][0].shape, jnp.bfloat16)
    return pl.pallas_call(
        functools.partial(pack_kernel, axes),
        out_shape=[shape] * len(axes),
        in_specs=[SMEM] + [HBM] * (5 * len(axes)),
        out_specs=[VMEM] * len(axes),
        scratch_shapes=[pltpu.SemaphoreType.DMA((5 * len(axes),))],
        compiler_params=pltpu.CompilerParams(vmem_limit_bytes=16 * MIB),
    )(place, *[piece for group in rings for piece in group])


def gather(place, blocks):
    firsts = [first for _, first, _ in blocks]
    slabs = pack(place, firsts, [(b,) + ring(b, first) for b, first, _ in blocks])
    pieces = []
    for slab, (_, first, column) in zip(slabs, blocks):
        axis = "z" if first == "y" else "y"
        below, above, low, high = ring(slab, axis)
        pieces += [
            (slab, axis, 0, 0, column),
            (below, axis, 3, 0, column),
            (above, axis, 1, 0, column),
            (low, axis, 2, 0, column),
            (high, axis, 2, SIDE // 2, column),
        ]
    return pieces


def keep_pieces_kernel(plan, place, _, *refs):
    pieces, kept_ref, sems = refs[: len(plan)], refs[-2], refs[-1]
    copies = []
    for ref, (axis, distance, low, column) in zip(pieces, plan):
        run = pl.ds(low, ref.shape[0])
        if axis == "z":
            at = ((place[0] + distance) % SIDE, run)
        else:
            at = (run, (place[1] + distance) % SIDE)
        for n in range(column // TILE, (column + ref.shape[2]) // TILE):
            copies.append(
                pltpu.make_async_copy(
                    ref.at[:, :, pl.ds(n * TILE - column, TILE)],
                    kept_ref.at[(n,) + at],
                    sems.at[len(copies)],
                )
            )
    for copy in copies:
        copy.start()
    for copy in copies:
        copy.wait()


def keep_pieces(place, after, pieces, depth, tiles):
    plan = [entry[1:] for entry in pieces]
    kept = pl.pallas_call(
        functools.partial(keep_pieces_kernel, plan),
        out_shape=jax.ShapeDtypeStruct((tiles, SIDE, SIDE, depth, TILE), jnp.bfloat16),
        in_specs=[SMEM, VMEM] + [HBM] * len(plan),
        out_specs=VMEM,
        scratch_shapes=[pltpu.SemaphoreType.DMA((len(plan) * tiles,))],
        compiler_params=pltpu.CompilerParams(vmem_limit_bytes=PIECES_MIB * MIB),
    )(place, after, *[entry[0] for entry in pieces])
    return kept.reshape(tiles, SIDE * SIDE, depth, TILE)


def keep_kernel(whole_ref, kept_ref, k_ref, v_ref, sems):
    count, blocks, depth, tile = kept_ref.shape
    rows = k_ref.shape[1]
    chunk = whole_ref.shape[2]
    copies = [
        pltpu.make_async_copy(
            whole_ref.at[:, pl.ds(0, depth), pl.ds(n * tile, tile)], kept_ref.at[n], sems.at[n]
        )
        for n in range(count)
    ]
    start = depth
    for target in (k_ref, v_ref):
        for column in range(0, target.shape[2], chunk):
            copies.append(
                pltpu.make_async_copy(
                    whole_ref.at[:, pl.ds(start, rows)],
                    target.at[:, :, pl.ds(column, chunk)],
                    sems.at[len(copies)],
                )
            )
            start += rows
    for copy in copies:
        copy.start()
    for copy in copies:
        copy.wait()


def keep(whole, depth, width):
    blocks, block, chunk = whole.shape
    chunks = width // chunk
    rows = (block - depth) // (2 * chunks)
    caption = jax.ShapeDtypeStruct((blocks, rows, width), jnp.bfloat16)
    kept, keys, values = pl.pallas_call(
        keep_kernel,
        out_shape=[
            jax.ShapeDtypeStruct((chunk // TILE, blocks, depth, TILE), jnp.bfloat16),
            caption,
            caption,
        ],
        in_specs=[HBM],
        out_specs=[VMEM] * 3,
        scratch_shapes=[pltpu.SemaphoreType.DMA((chunk // TILE + 2 * chunks,))],
        compiler_params=pltpu.CompilerParams(vmem_limit_bytes=KEEP_MIB * MIB),
    )(whole)
    return kept, keys.reshape(blocks * rows, width), values.reshape(blocks * rows, width)


def attend_kernel(
    lengths, order, slot, x_ref, ring_ref, kept_ref, k_ref, v_ref, out_ref
):
    tokens, features = x_ref.shape
    blocks, depth = kept_ref.shape[1:3]
    early = ring_ref.shape[0]
    tiles = early + kept_ref.shape[0]
    sample = order[slot[0]]
    start = jnp.int32(0)
    for i in range(lengths.shape[0] - 1):
        start = start + jnp.where(i < sample, lengths[i], 0)
    stop = start + lengths[sample]
    base = pl.multiple_of(jnp.minimum(start // 16 * 16, k_ref.shape[0] - WINDOW), 16)
    row = base + lax.broadcasted_iota(jnp.int32, (1, WINDOW), 1)
    valid = (row >= start) & (row < stop)
    step = 512
    squares = jnp.zeros((tokens, step), jnp.float32)
    for at in range(0, features, step):
        xf = x_ref[:, at : at + step].astype(jnp.float32)
        squares = squares + xf * xf
    scale = lax.rsqrt(jnp.sum(squares, axis=-1, keepdims=True) / features + 1e-06)
    query = None
    for n in range(tiles):
        weight = ring_ref[n] if n < early else kept_ref[n - early]
        weight = weight.reshape(blocks * depth, TILE)
        product = jnp.dot(x_ref[...], weight, preferred_element_type=jnp.float32)
        if n > 0:
            attend_tile(n - 1, query, valid, base, k_ref, v_ref, out_ref)
        query = (product * scale).astype(jnp.bfloat16)
    attend_tile(tiles - 1, query, valid, base, k_ref, v_ref, out_ref)


def attend(lengths, order, slot, x, ring_tiles, kept, keys, values):
    tokens, features = x.shape
    width = keys.shape[1]
    return pl.pallas_call(
        attend_kernel,
        out_shape=jax.ShapeDtypeStruct((tokens, width), jnp.bfloat16),
        in_specs=[SMEM] * 3 + [VMEM] * 5,
        out_specs=VMEM,
        compiler_params=pltpu.CompilerParams(vmem_limit_bytes=ATTEND_MIB * MIB),
        cost_estimate=pl.CostEstimate(
            flops=2 * tokens * features * width,
            bytes_accessed=2 * features * width,
            transcendentals=0,
        ),
    )(lengths, order, slot, x, ring_tiles, kept, keys, values)


ATTEND_MIB = 8
PIECES_MIB = 8
KEEP_MIB = 16


def hold_kernel(src_ref, dst_ref, sem):
    copy = pltpu.make_async_copy(src_ref, dst_ref, sem)
    copy.start()
    copy.wait()


def hold(w):
    return pl.pallas_call(
        hold_kernel,
        out_shape=jax.ShapeDtypeStruct(w.shape, w.dtype),
        in_specs=[HBM],
        out_specs=VMEM,
        scratch_shapes=[pltpu.SemaphoreType.DMA],
        compiler_params=pltpu.CompilerParams(vmem_limit_bytes=1 * MIB),
    )(w)


def project_kernel(column, a_ref, w_ref, x_ref, out_ref):
    tile = 512

    @pl.loop(0, out_ref.shape[1] // tile)
    def _(n):
        cols = pl.ds(pl.multiple_of(n * tile, tile), tile)
        from_cols = pl.ds(pl.multiple_of(column + n * tile, tile), tile)
        p = jnp.dot(a_ref[...], w_ref[:, from_cols], preferred_element_type=jnp.float32)
        out_ref[:, cols] = (x_ref[:, cols].astype(jnp.float32) + p).astype(jnp.bfloat16)


def project(attended, w, x, column):
    return pl.pallas_call(
        functools.partial(project_kernel, column),
        out_shape=jax.ShapeDtypeStruct(x.shape, jnp.bfloat16),
        in_specs=[VMEM] * 3,
        out_specs=VMEM,
        compiler_params=pltpu.CompilerParams(vmem_limit_bytes=4 * MIB),
        cost_estimate=pl.CostEstimate(
            flops=2 * x.shape[0] * w.shape[0] * x.shape[1],
            bytes_accessed=2 * w.shape[0] * x.shape[1],
            transcendentals=0,
        ),
    )(attended, w, x)


def body(video, caption_kv, caption_lengths, order, gains, w_query, w_out):
    samples = video.shape[0]
    segments = lax.axis_size("segment")
    here = lax.axis_index("segment")
    seq = lax.axis_index("seq")
    depth, width = w_query.shape[1:]

    gain = lax.dynamic_slice_in_dim(gains[0], seq * depth, depth)
    weight = (w_query[0].astype(jnp.float32) * gain[:, None]).astype(jnp.bfloat16)
    third = width // 3
    early = width - third
    captions = [
        caption_kv[0, :, i, c : c + third] for i in range(2) for c in range(0, width, third)
    ]
    local = jnp.concatenate([weight[:, early:]] + captions, axis=0)
    gathered = lax.all_gather(local, "seq", axis=0)
    place = jnp.stack([seq // SIDE, seq % SIDE]).astype(jnp.int32)
    blocks = [(weight[:, : early // 2], "y", 0), (weight[:, early // 2 : early], "z", early // 2)]
    kept, keys, values = keep(gathered, depth, width)
    ring_tiles = keep_pieces(place, kept, gather(place, blocks), depth, early // TILE)

    out_weight = hold(w_out[0])
    received = None
    results = []
    last = samples + segments - 2
    for tick in range(last + 1):
        slot = jnp.clip(tick - here, 0, samples - 1).astype(jnp.int32)[None]
        if tick < samples:
            current = lax.dynamic_index_in_dim(video, order[tick], 0, keepdims=False)
            if tick:
                current = jnp.where(here == 0, current, received)
        else:
            current = received
        whole = lax.all_gather(current, "mp", axis=1, tiled=True)
        attended = attend(caption_lengths, order, slot, whole, ring_tiles, kept, keys, values)
        attended = lax.all_gather(attended, "mp", axis=1, tiled=True)
        mixed = project(attended, out_weight, current, 0)
        if tick < last:
            received = lax.ppermute(
                mixed, "segment", [(i, i + 1) for i in range(segments - 1)]
            )
        results.append(mixed)
    stacked = jnp.stack(results)
    return lax.dynamic_slice_in_dim(stacked, here, samples, 0)[None]


def solution(mesh):
    in_specs = (
        P(None, "seq", "mp"),
        P("segment", "seq", None, "mp"),
        P(),
        P(),
        P("segment", None),
        P("segment", "seq", "mp"),
        P("segment", None, "mp"),
    )
    out_specs = P("segment", None, "seq", "mp")
    return jax.shard_map(body, mesh=mesh, in_specs=in_specs, out_specs=out_specs, check_vma=False)
```

time: 331 us -> 316 us (0.955)
  waiting for transfers between devices: 185 us -> 106 us
  local copies, waits for them, and re-layouts: 3.75 us -> 38.5 us
  starting transfers between devices: 15.5 us -> 37.3 us
  blocking collectives: 31.9 us -> 44.3 us
  Pallas kernels: 69.1 us -> 63.5 us
    all_gather x1, waiting for transfers between devices: 140 us -> 3.87 us  [body(): gathered = lax.all_gather(local, 'seq', axis=0)]
    ppermute x0 -> x16, waiting for transfers between devices: none -> 56.7 us  [shift(): return lax.ppermute(block, 'seq', pairs)]
    unnamed x27 -> x68, local copies, waits for them, and re-layouts: 0.19 us -> 25.9 us
    ppermute x0 -> x16, starting transfers between devices: none -> 21.8 us  [shift(): return lax.ppermute(block, 'seq', pairs)]
    pallas_call x6, Pallas kernels: 42.3 us -> 31.9 us  [attend(): pl.pallas_call(attend_kernel, out_shape=jax.ShapeDtypeStruct((tokens, wid...]
    all_gather x6, blocking collectives: 19 us -> 29 us  [body(): whole = lax.all_gather(current, 'mp', axis=1, tiled=True)]
    slice x1 -> x10, local copies, waits for them, and re-layouts: 1.67 us -> 10.1 us  [the longest x4 4.48 us: ring(): below[:half]]
    pallas_call x1 -> x4, Pallas kernels: 6.62 us -> 11.4 us  [the longest x1 4.75 us: keep_pieces(): pl.pallas_call(functools.partial(keep_pieces_kernel, plan), out_shape=jax...]
  transfers between devices with their start and end apart: 6 -> 22, of which waited for: 6 -> 13; matrix products, arithmetic and copies ran while one was open for 0% -> 3% of each run, Pallas kernels for 0% -> 2%
where the time goes in v2:
time: 316 us; the launch traced here: 315 us
  waiting for transfers between devices  106 us (34%)
  Pallas kernels  63.5 us (20%)
  blocking collectives  44.3 us (14%)
  local copies, waits for them, and re-layouts  38.5 us (12%)
  starting transfers between devices  37.3 us (12%)
  between operations  19.5 us (6%)
  other arithmetic  5.73 us (2%)
    ppermute x16, waiting for transfers between devices, shift(): return lax.ppermute(block, 'seq', pairs)  56.7 us
    ppermute x5, waiting for transfers between devices, body(): lax.ppermute(mixed, 'segment', [(i, i + 1) for i in range(segments - 1)])  45.3 us
    pallas_call x6, Pallas kernels, attend(): pl.pallas_call(attend_kernel, out_shape=jax.ShapeDtypeStruct((tokens, wid...  31.9 us
    all_gather x6, blocking collectives, body(): whole = lax.all_gather(current, 'mp', axis=1, tiled=True)  29 us
    unnamed x68, local copies, waits for them, and re-layouts  25.9 us
    ppermute x16, starting transfers between devices, shift(): return lax.ppermute(block, 'seq', pairs)  21.8 us
    pallas_call x5, Pallas kernels, project(): pl.pallas_call(functools.partial(project_kernel, column), out_shape=jax.S...  20.2 us
    ppermute x5, starting transfers between devices, body(): lax.ppermute(mixed, 'segment', [(i, i + 1) for i in range(segments - 1)])  15.5 us
  transfers between devices with their start and end apart: 22, of which 13 were waited for; matrix products, arithmetic and copies ran while one was open for 3% of the time, Pallas kernels for 2%

profile of v2, /device:TPU:3, one launch (start us, length us, event | category | flops | bytes accessed | tf_op | source)
XLA Modules:
  0.0 314.9 jit_solution(10734421638762405597)
XLA Ops:
  10.9 3.8 %collective-permute-start.5 = (bf16[384,512]{1,0:T(8,128)(2,1)S(1)}, bf16[384,512]{1,0:T(8,128)(2,1)S(1)}, u32[]{:S(2)}, u32[]{:S(2)}) collective-permute-start(bf16[384,512]{1,0:T(8,128)(2,1)S(1)} %get-tuple-element.15.refs_5_), channel_id=1, source_target_pairs={{0,24},{2,26},{4,28},{6,30},{8,0},{10,2},{12,4},{14,6},{16,8},{18,... | collective-permute-start | bytes 1179656 | tf_op jit(solution)/shard_map/ppermute | solution.py:57
  17.4 5.0 %collective-permute-done.5.refs_7_ = bf16[384,512]{1,0:T(8,128)(2,1)S(1)} collective-permute-done((bf16[384,512]{1,0:T(8,128)(2,1)S(1)}, bf16[384,512]{1,0:T(8,128)(2,1)S(1)}, u32[]{:S(2)}, u32[]{:S(2)}) %collective-permute-start.5) | collective-permute-done | bytes 393248 | tf_op jit(solution)/shard_map/ppermute | solution.py:57
  22.5 3.5 %collective-permute-start.7 = (bf16[192,512]{1,0:T(8,128)(2,1)S(1)}, bf16[192,512]{1,0:T(8,128)(2,1)S(1)}, u32[]{:S(2)}, u32[]{:S(2)}) collective-permute-start(bf16[192,512]{1,0:T(8,128)(2,1)S(1)} %slice.86), channel_id=1, source_target_pairs={{0,24},{2,26},{4,28},{6,30},{8,0},{10,2},{12,4},{14,6},{16,8},{18,... | collective-permute-start | bytes 589832 | tf_op jit(solution)/shard_map/ppermute | solution.py:57
  37.5 4.5 %collective-permute-done.2.refs_3_ = bf16[192,512]{1,0:T(8,128)(2,1)S(1)} collective-permute-done((bf16[192,512]{1,0:T(8,128)(2,1)}, bf16[192,512]{1,0:T(8,128)(2,1)S(1)}, u32[]{:S(2)}, u32[]{:S(2)}) %collective-permute-start.2) | collective-permute-done | bytes 196640 | tf_op jit(solution)/shard_map/ppermute | solution.py:57
  41.9 4.5 %shard_map.74 = (bf16[4,384,512]{2,1,0:T(8,128)(2,1)}, bf16[4,384,512]{2,1,0:T(8,128)(2,1)}) custom-call(s32[2]{0:T(128)S(1)} %pad_add_fusion.place, bf16[384,512]{1,0:T(8,128)(2,1)S(1)} %get-tuple-element.16.refs_0_, bf16[384,512]{1,0:T(8,128)(2,1)S(1)} %collective-permute-done.refs_1_, bf16[384,512]{1,0:T(8,128)(2,1)S(1)} %collective-permute-done.1.refs_2_, ...), custom_call_target="tpu_custom_call" | custom-call | tf_op jit(solution)/shard_map/pallas_call | solution.py:91
  55.0 6.4 %copy-done.7 = bf16[1,3072,3072]{2,1,0:T(8,128)(2,1)S(1)} copy-done((bf16[1,3072,3072]{2,1,0:T(8,128)(2,1)S(1)}, bf16[1,3072,3072]{2,1,0:T(8,128)(2,1)}, u32[]{:S(2)}) %copy-start.7) | copy-done | bytes 18874392
  62.7 6.4 %copy-done.2 = bf16[3072,3072]{1,0:T(8,128)(2,1)} copy-done((bf16[3072,3072]{1,0:T(8,128)(2,1)}, bf16[3072,3072]{1,0:T(8,128)(2,1)S(1)}, u32[]{:S(2)}) %copy-start.2) | copy-done | bytes 18874392
  71.0 39.5 %collective-permute-done.9.refs_2_ = bf16[4,384,512]{2,1,0:T(8,128)(2,1)S(1)} collective-permute-done((bf16[4,384,512]{2,1,0:T(8,128)(2,1)}, bf16[4,384,512]{2,1,0:T(8,128)(2,1)S(1)}, u32[]{:S(2)}, u32[]{:S(2)}) %collective-permute-start.9) | collective-permute-done | bytes 1572896 | tf_op jit(solution)/shard_map/ppermute | solution.py:57
  121.7 12.6 %all-gather = bf16[1,64,6144]{2,1,0:T(8,128)(2,1)} all-gather(bf16[1,64,3072]{2,1,0:T(8,128)(2,1)S(1)} %constant_dynamic-slice_fusion), channel_id=2, replica_groups=mesh['segment'=4,'seq'=16,'mp'=2] {'mp'}, dimensions={2}, use_global_device_ids=true | all-gather | bytes 1179648 | tf_op jit(solution)/shard_map/all_gather | solution.py:331
  135.0 3.9 %all-gather.4.cloned.1.call-done = bf16[10752,512]{1,0:T(8,128)(2,1)} async-done(((bf16[672,512]{1,0:T(8,128)(2,1)}), bf16[10752,512]{1,0:T(8,128)(2,1)}) %all-gather.4.cloned.1.call-update) | async-done | bytes 11010064 | tf_op jit(solution)/shard_map/all_gather | solution.py:313
  138.9 4.1 %copy-done.8 = bf16[10752,512]{1,0:T(8,128)(2,1)S(1)} copy-done((bf16[10752,512]{1,0:T(8,128)(2,1)S(1)}, bf16[10752,512]{1,0:T(8,128)(2,1)}, u32[]{:S(2)}) %copy-start.8) | copy-done | bytes 11010072
  147.6 4.8 %shard_map.75 = bf16[4,4,4,384,256]{4,3,2,1,0:T(8,128)(2,1)S(1)} custom-call(s32[2]{0:T(128)S(1)} %pad_add_fusion.place, bf16[2,16,384,256]{3,2,1,0:T(8,128)(2,1)S(1)} %get-tuple-element.10._.kept_ref, bf16[4,384,512]{2,1,0:T(8,128)(2,1)} %get-tuple-element.11.refs_0_, bf16[4,384,512]{2,1,0:T(8,128)(2,1)S(1)} %copy-done.12, ...), custom_call_target="tpu_custom_call" | custom-call | tf_op jit(solution)/shard_map/pallas_call | solution.py:143
  152.4 3.5 %copy-done.4 = bf16[2,16,384,256]{3,2,1,0:T(8,128)(2,1)S(1)} copy-done((bf16[2,16,384,256]{3,2,1,0:T(8,128)(2,1)S(1)}, bf16[2,16,384,256]{3,2,1,0:T(8,128)(2,1)}, u32[]{:S(2)}) %copy-start.4) | copy-done | bytes 6291480
  157.6 5.4 %shard_map.76 = bf16[64,1536]{1,0:T(8,128)(2,1)S(1)} custom-call(s32[3]{0:T(128)S(1)} %copy-done.18, s32[3]{0:T(128)S(1)} %copy-done.17, s32[1]{0:T(128)} %bitcast.slot, bf16[64,6144]{1,0:T(8,128)(2,1)S(1)} %bitcast.88, bf16[4,16,384,256]{3,2,1,0:T(8,128)(2,1)S(1)} %bitcast.66, bf16[2,16,384,256]{3,2,1,0:T(8,128)(2,1)S(1)} %copy-done.4, ...), custom_call_target="tpu_custom_call" | custom-call | flops 1207959552 | bytes 18874368 | tf_op jit(solution)/shard_map/pallas_call | solution.py:236
  163.0 4.8 %all_gather.45.a_ref = bf16[64,3072]{1,0:T(8,128)(2,1)S(1)} all-gather(bf16[64,1536]{1,0:T(8,128)(2,1)S(1)} %shard_map.76), channel_id=1, replica_groups=mesh['segment'=4,'seq'=16,'mp'=2] {'mp'}, dimensions={1}, use_global_device_ids=true | all-gather | bytes 589824 | tf_op jit(solution)/shard_map/all_gather | solution.py:333
  167.9 4.0 %shard_map.78 = bf16[64,3072]{1,0:T(8,128)(2,1)S(1)} custom-call(bf16[64,3072]{1,0:T(8,128)(2,1)S(1)} %all_gather.45.a_ref, bf16[3072,3072]{1,0:T(8,128)(2,1)S(1)} %bitcast.65, bf16[64,3072]{1,0:T(8,128)(2,1)S(1)} %copy-done.14), custom_call_target="tpu_custom_call" | custom-call | flops 1207959552 | bytes 18874368 | tf_op jit(solution)/shard_map/pallas_call | solution.py:284
  175.1 9.1 %collective-permute-done.16 = bf16[64,3072]{1,0:T(8,128)(2,1)S(1)} collective-permute-done((bf16[64,3072]{1,0:T(8,128)(2,1)S(1)}, bf16[64,3072]{1,0:T(8,128)(2,1)S(1)}, u32[]{:S(2)}, u32[]{:S(2)}) %collective-permute-start.16) | collective-permute-done | bytes 393248 | tf_op jit(solution)/shard_map/ppermute | solution.py:336
  187.5 5.3 %shard_map.79 = bf16[64,1536]{1,0:T(8,128)(2,1)S(1)} custom-call(s32[3]{0:T(128)S(1)} %copy-done.18, s32[3]{0:T(128)S(1)} %copy-done.17, s32[1]{0:T(128)} %bitcast.19.slot, bf16[64,6144]{1,0:T(8,128)(2,1)S(1)} %all_gather.46.x_ref, bf16[4,16,384,256]{3,2,1,0:T(8,128)(2,1)S(1)} %bitcast.67, bf16[2,16,384,256]{3,2,1,0:T(8,128)(2,1)S(1)} %bitcast.73, ...), custom_call_target="tpu_custom_call" | custom-call | flops 1207959552 | bytes 18874368 | tf_op jit(solution)/shard_map/pallas_call | solution.py:236
  194.9 4.0 %shard_map.80 = bf16[64,3072]{1,0:T(8,128)(2,1)S(1)} custom-call(bf16[64,3072]{1,0:T(8,128)(2,1)S(1)} %all_gather.47.a_ref, bf16[3072,3072]{1,0:T(8,128)(2,1)S(1)} %bitcast.65, bf16[64,3072]{1,0:T(8,128)(2,1)S(1)} %bitcast_select_fusion.1.x_ref), custom_call_target="tpu_custom_call" | custom-call | flops 1207959552 | bytes 18874368 | tf_op jit(solution)/shard_map/pallas_call | solution.py:284
  202.1 9.1 %collective-permute-done.17 = bf16[64,3072]{1,0:T(8,128)(2,1)S(1)} collective-permute-done((bf16[64,3072]{1,0:T(8,128)(2,1)S(1)}, bf16[64,3072]{1,0:T(8,128)(2,1)S(1)}, u32[]{:S(2)}, u32[]{:S(2)}) %collective-permute-start.17) | collective-permute-done | bytes 393248 | tf_op jit(solution)/shard_map/ppermute | solution.py:336
  214.6 5.3 %shard_map.81 = bf16[64,1536]{1,0:T(8,128)(2,1)S(1)} custom-call(s32[3]{0:T(128)S(1)} %copy-done.18, s32[3]{0:T(128)S(1)} %copy-done.17, s32[1]{0:T(128)} %bitcast.23.slot, bf16[64,6144]{1,0:T(8,128)(2,1)S(1)} %all_gather.48.x_ref, bf16[4,16,384,256]{3,2,1,0:T(8,128)(2,1)S(1)} %bitcast.68, bf16[2,16,384,256]{3,2,1,0:T(8,128)(2,1)S(1)} %bitcast.73, ...), custom_call_target="tpu_custom_call" | custom-call | flops 1207959552 | bytes 18874368 | tf_op jit(solution)/shard_map/pallas_call | solution.py:236
  222.0 4.0 %shard_map.82 = bf16[64,3072]{1,0:T(8,128)(2,1)S(1)} custom-call(bf16[64,3072]{1,0:T(8,128)(2,1)S(1)} %all_gather.49.a_ref, bf16[3072,3072]{1,0:T(8,128)(2,1)S(1)} %bitcast.65, bf16[64,3072]{1,0:T(8,128)(2,1)S(1)} %bitcast_select_fusion.x_ref), custom_call_target="tpu_custom_call" | custom-call | flops 1207959552 | bytes 18874368 | tf_op jit(solution)/shard_map/pallas_call | solution.py:284
  229.2 9.1 %collective-permute-done.18.x_ref = bf16[64,3072]{1,0:T(8,128)(2,1)S(1)} collective-permute-done((bf16[64,3072]{1,0:T(8,128)(2,1)S(1)}, bf16[64,3072]{1,0:T(8,128)(2,1)S(1)}, u32[]{:S(2)}, u32[]{:S(2)}) %collective-permute-start.18) | collective-permute-done | bytes 393248 | tf_op jit(solution)/shard_map/ppermute | solution.py:336
  241.5 5.3 %shard_map.83 = bf16[64,1536]{1,0:T(8,128)(2,1)S(1)} custom-call(s32[3]{0:T(128)S(1)} %copy-done.18, s32[3]{0:T(128)S(1)} %copy-done.17, s32[1]{0:T(128)} %bitcast.27.slot, bf16[64,6144]{1,0:T(8,128)(2,1)S(1)} %all_gather.50.x_ref, bf16[4,16,384,256]{3,2,1,0:T(8,128)(2,1)S(1)} %bitcast.69, bf16[2,16,384,256]{3,2,1,0:T(8,128)(2,1)S(1)} %bitcast.73, ...), custom_call_target="tpu_custom_call" | custom-call | flops 1207959552 | bytes 18874368 | tf_op jit(solution)/shard_map/pallas_call | solution.py:236
  248.9 4.0 %shard_map.84 = bf16[64,3072]{1,0:T(8,128)(2,1)S(1)} custom-call(bf16[64,3072]{1,0:T(8,128)(2,1)S(1)} %all_gather.51.a_ref, bf16[3072,3072]{1,0:T(8,128)(2,1)S(1)} %bitcast.65, bf16[64,3072]{1,0:T(8,128)(2,1)S(1)} %collective-permute-done.18.x_ref), custom_call_target="tpu_custom_call" | custom-call | flops 1207959552 | bytes 18874368 | tf_op jit(solution)/shard_map/pallas_call | solution.py:284
  256.1 9.1 %collective-permute-done.19.x_ref = bf16[64,3072]{1,0:T(8,128)(2,1)S(1)} collective-permute-done((bf16[64,3072]{1,0:T(8,128)(2,1)S(1)}, bf16[64,3072]{1,0:T(8,128)(2,1)S(1)}, u32[]{:S(2)}, u32[]{:S(2)}) %collective-permute-start.19) | collective-permute-done | bytes 393248 | tf_op jit(solution)/shard_map/ppermute | solution.py:336
  265.1 3.4 %all_gather.52.x_ref = bf16[64,6144]{1,0:T(8,128)(2,1)S(1)} all-gather(bf16[64,3072]{1,0:T(8,128)(2,1)S(1)} %collective-permute-done.19.x_ref), channel_id=1, replica_groups=mesh['segment'=4,'seq'=16,'mp'=2] {'mp'}, dimensions={1}, use_global_device_ids=true | all-gather | bytes 1179648 | tf_op jit(solution)/shard_map/all_gather | solution.py:331
  268.6 5.3 %shard_map.85 = bf16[64,1536]{1,0:T(8,128)(2,1)S(1)} custom-call(s32[3]{0:T(128)S(1)} %copy-done.18, s32[3]{0:T(128)S(1)} %copy-done.17, s32[1]{0:T(128)} %bitcast.29.slot, bf16[64,6144]{1,0:T(8,128)(2,1)S(1)} %all_gather.52.x_ref, bf16[4,16,384,256]{3,2,1,0:T(8,128)(2,1)S(1)} %bitcast.70, bf16[2,16,384,256]{3,2,1,0:T(8,128)(2,1)S(1)} %bitcast.73, ...), custom_call_target="tpu_custom_call" | custom-call | flops 1207959552 | bytes 18874368 | tf_op jit(solution)/shard_map/pallas_call | solution.py:236
  276.0 4.0 %shard_map.86 = bf16[64,3072]{1,0:T(8,128)(2,1)S(1)} custom-call(bf16[64,3072]{1,0:T(8,128)(2,1)S(1)} %all_gather.53.a_ref, bf16[3072,3072]{1,0:T(8,128)(2,1)S(1)} %bitcast.65, bf16[64,3072]{1,0:T(8,128)(2,1)S(1)} %collective-permute-done.19.x_ref), custom_call_target="tpu_custom_call" | custom-call | flops 1207959552 | bytes 18874368 | tf_op jit(solution)/shard_map/pallas_call | solution.py:284
  283.2 9.1 %collective-permute-done.20 = bf16[64,3072]{1,0:T(8,128)(2,1)S(1)} collective-permute-done((bf16[64,3072]{1,0:T(8,128)(2,1)S(1)}, bf16[64,3072]{1,0:T(8,128)(2,1)S(1)}, u32[]{:S(2)}, u32[]{:S(2)}) %collective-permute-start.20) | collective-permute-done | bytes 393248 | tf_op jit(solution)/shard_map/ppermute | solution.py:336
  295.4 5.3 %shard_map.87 = bf16[64,1536]{1,0:T(8,128)(2,1)S(1)} custom-call(s32[3]{0:T(128)S(1)} %copy-done.18, s32[3]{0:T(128)S(1)} %copy-done.17, s32[1]{0:T(128)} %bitcast.31.slot, bf16[64,6144]{1,0:T(8,128)(2,1)S(1)} %all_gather.54.x_ref, bf16[4,16,384,256]{3,2,1,0:T(8,128)(2,1)S(1)} %bitcast.71, bf16[2,16,384,256]{3,2,1,0:T(8,128)(2,1)S(1)} %bitcast.73, ...), custom_call_target="tpu_custom_call" | custom-call | flops 1207959552 | bytes 18874368 | tf_op jit(solution)/shard_map/pallas_call | solution.py:236
  302.9 4.0 %shard_map.88 = bf16[6,64,3072]{2,1,0:T(8,128)(2,1)S(1)} fusion(bf16[6,64,3072]{2,1,0:T(8,128)(2,1)S(1)} %bitcast_dynamic-update-slice_fusion.1, bf16[64,3072]{1,0:T(8,128)(2,1)S(1)} %all_gather.55, bf16[3072,3072]{1,0:T(8,128)(2,1)S(1)} %bitcast.65, bf16[64,3072]{1,0:T(8,128)(2,1)S(1)} %collective-permute-done.20), kind=kCustom, calls=%fused_computation.4 | custom fusion | flops 1207959552 | bytes 20054016 | tf_op jit(solution)/shard_map/pallas_call | solution.py:284
  (131 shorter events, 83.1 us)
Async XLA Ops:
  6.5 132.4 %all-gather.4.cloned.1.call-start = ((), (), s32[]{:S(2)}) async-start(), calls=%async_computation | async-start | bytes 11698176 | tf_op jit(solution)/shard_map/all_gather | solution.py:313
  10.9 11.6 %collective-permute-start.5 = (bf16[384,512]{1,0:T(8,128)(2,1)S(1)}, bf16[384,512]{1,0:T(8,128)(2,1)S(1)}, u32[]{:S(2)}, u32[]{:S(2)}) collective-permute-start(bf16[384,512]{1,0:T(8,128)(2,1)S(1)} %get-tuple-element.15.refs_5_), channel_id=1, source_target_pairs={{0,24},{2,26},{4,28},{6,30},{8,0},{10,2},{12,4},{14,6},{16,8},{18,... | collective-permute-start | bytes 1179656 | tf_op jit(solution)/shard_map/ppermute | solution.py:57
  14.7 11.3 %collective-permute-start.4 = (bf16[384,512]{1,0:T(8,128)(2,1)S(1)}, bf16[384,512]{1,0:T(8,128)(2,1)S(1)}, u32[]{:S(2)}, u32[]{:S(2)}) collective-permute-start(bf16[384,512]{1,0:T(8,128)(2,1)S(1)} %get-tuple-element.15.refs_5_), channel_id=1, source_target_pairs={{0,8},{2,10},{4,12},{6,14},{8,16},{10,18},{12,20},{14,22},{16,24},... | collective-permute-start | bytes 1179656 | tf_op jit(solution)/shard_map/ppermute | solution.py:57
  14.7 35.9 %copy-start.17 = (s32[3]{0:T(128)S(1)}, s32[3]{0:T(128)}, u32[]{:S(2)}) copy-start(s32[3]{0:T(128)} %order.11) | copy-start | bytes 40
  14.7 12.0 %collective-permute-start.1 = (bf16[384,512]{1,0:T(8,128)(2,1)S(1)}, bf16[384,512]{1,0:T(8,128)(2,1)S(1)}, u32[]{:S(2)}, u32[]{:S(2)}) collective-permute-start(bf16[384,512]{1,0:T(8,128)(2,1)S(1)} %get-tuple-element.16.refs_0_), channel_id=1, source_target_pairs={{0,6},{2,0},{4,2},{6,4},{8,14},{10,8},{12,10},{14,12},{16,22},{18,... | collective-permute-start | bytes 1179656 | tf_op jit(solution)/shard_map/ppermute | solution.py:57
  17.4 12.7 %collective-permute-start = (bf16[384,512]{1,0:T(8,128)(2,1)S(1)}, bf16[384,512]{1,0:T(8,128)(2,1)S(1)}, u32[]{:S(2)}, u32[]{:S(2)}) collective-permute-start(bf16[384,512]{1,0:T(8,128)(2,1)S(1)} %get-tuple-element.16.refs_0_), channel_id=1, source_target_pairs={{0,2},{2,4},{4,6},{6,0},{8,10},{10,12},{12,14},{14,8},{16,18},{18,... | collective-permute-start | bytes 1179656 | tf_op jit(solution)/shard_map/ppermute | solution.py:57
  22.5 11.5 %collective-permute-start.7 = (bf16[192,512]{1,0:T(8,128)(2,1)S(1)}, bf16[192,512]{1,0:T(8,128)(2,1)S(1)}, u32[]{:S(2)}, u32[]{:S(2)}) collective-permute-start(bf16[192,512]{1,0:T(8,128)(2,1)S(1)} %slice.86), channel_id=1, source_target_pairs={{0,24},{2,26},{4,28},{6,30},{8,0},{10,2},{12,4},{14,6},{16,8},{18,... | collective-permute-start | bytes 589832 | tf_op jit(solution)/shard_map/ppermute | solution.py:57
  26.7 9.9 %collective-permute-start.6 = (bf16[192,512]{1,0:T(8,128)(2,1)}, bf16[192,512]{1,0:T(8,128)(2,1)S(1)}, u32[]{:S(2)}, u32[]{:S(2)}) collective-permute-start(bf16[192,512]{1,0:T(8,128)(2,1)} %slice.85), channel_id=1, source_target_pairs={{0,8},{2,10},{4,12},{6,14},{8,16},{10,18},{12,20},{14,22},{16,24},... | collective-permute-start | bytes 589832 | tf_op jit(solution)/shard_map/ppermute | solution.py:57
  27.4 10.1 %collective-permute-start.3 = (bf16[192,512]{1,0:T(8,128)(2,1)}, bf16[192,512]{1,0:T(8,128)(2,1)S(1)}, u32[]{:S(2)}, u32[]{:S(2)}) collective-permute-start(bf16[192,512]{1,0:T(8,128)(2,1)} %slice.83), channel_id=1, source_target_pairs={{0,6},{2,0},{4,2},{6,4},{8,14},{10,8},{12,10},{14,12},{16,22},{18,... | collective-permute-start | bytes 589832 | tf_op jit(solution)/shard_map/ppermute | solution.py:57
  30.8 11.1 %collective-permute-start.2 = (bf16[192,512]{1,0:T(8,128)(2,1)}, bf16[192,512]{1,0:T(8,128)(2,1)S(1)}, u32[]{:S(2)}, u32[]{:S(2)}) collective-permute-start(bf16[192,512]{1,0:T(8,128)(2,1)} %slice.82), channel_id=1, source_target_pairs={{0,2},{2,4},{4,6},{6,0},{8,10},{10,12},{12,14},{14,8},{16,18},{18,... | collective-permute-start | bytes 589832 | tf_op jit(solution)/shard_map/ppermute | solution.py:57
  46.5 64.0 %collective-permute-start.9 = (bf16[4,384,512]{2,1,0:T(8,128)(2,1)}, bf16[4,384,512]{2,1,0:T(8,128)(2,1)S(1)}, u32[]{:S(2)}, u32[]{:S(2)}) collective-permute-start(bf16[4,384,512]{2,1,0:T(8,128)(2,1)} %get-tuple-element.11.refs_0_), channel_id=1, source_target_pairs={{0,24},{2,26},{4,28},{6,30},{8,0},{10,2},{12,4},{14,6},{16,8},{18,... | collective-permute-start | bytes 4718600 | tf_op jit(solution)/shard_map/ppermute | solution.py:57
  49.1 65.8 %collective-permute-start.8 = (bf16[4,384,512]{2,1,0:T(8,128)(2,1)}, bf16[4,384,512]{2,1,0:T(8,128)(2,1)S(1)}, u32[]{:S(2)}, u32[]{:S(2)}) collective-permute-start(bf16[4,384,512]{2,1,0:T(8,128)(2,1)} %get-tuple-element.11.refs_0_), channel_id=1, source_target_pairs={{0,8},{2,10},{4,12},{6,14},{8,16},{10,18},{12,20},{14,22},{16,24},... | collective-permute-start | bytes 4718600 | tf_op jit(solution)/shard_map/ppermute | solution.py:57
  49.1 66.9 %collective-permute-start.13 = (bf16[4,384,512]{2,1,0:T(8,128)(2,1)}, bf16[4,384,512]{2,1,0:T(8,128)(2,1)}, u32[]{:S(2)}, u32[]{:S(2)}) collective-permute-start(bf16[4,384,512]{2,1,0:T(8,128)(2,1)} %get-tuple-element.12.refs_5_), channel_id=1, source_target_pairs={{0,6},{2,0},{4,2},{6,4},{8,14},{10,8},{12,10},{14,12},{16,22},{18,... | collective-permute-start | bytes 4718600 | tf_op jit(solution)/shard_map/ppermute | solution.py:57
  49.1 68.9 %collective-permute-start.12 = (bf16[4,384,512]{2,1,0:T(8,128)(2,1)}, bf16[4,384,512]{2,1,0:T(8,128)(2,1)}, u32[]{:S(2)}, u32[]{:S(2)}) collective-permute-start(bf16[4,384,512]{2,1,0:T(8,128)(2,1)} %get-tuple-element.12.refs_5_), channel_id=1, source_target_pairs={{0,2},{2,4},{4,6},{6,0},{8,10},{10,12},{12,14},{14,8},{16,18},{18,... | collective-permute-start | bytes 4718600 | tf_op jit(solution)/shard_map/ppermute | solution.py:57
  111.5 32.4 %collective-permute-start.11 = (bf16[2,384,512]{2,1,0:T(8,128)(2,1)}, bf16[2,384,512]{2,1,0:T(8,128)(2,1)}, u32[]{:S(2)}, u32[]{:S(2)}) collective-permute-start(bf16[2,384,512]{2,1,0:T(8,128)(2,1)} %slice.88), channel_id=1, source_target_pairs={{0,24},{2,26},{4,28},{6,30},{8,0},{10,2},{12,4},{14,6},{16,8},{18,... | collective-permute-start | bytes 2359304 | tf_op jit(solution)/shard_map/ppermute | solution.py:57
  116.0 29.0 %collective-permute-start.10 = (bf16[2,384,512]{2,1,0:T(8,128)(2,1)}, bf16[2,384,512]{2,1,0:T(8,128)(2,1)}, u32[]{:S(2)}, u32[]{:S(2)}) collective-permute-start(bf16[2,384,512]{2,1,0:T(8,128)(2,1)} %slice.87), channel_id=1, source_target_pairs={{0,8},{2,10},{4,12},{6,14},{8,16},{10,18},{12,20},{14,22},{16,24},... | collective-permute-start | bytes 2359304 | tf_op jit(solution)/shard_map/ppermute | solution.py:57
  118.1 26.9 %collective-permute-start.15 = (bf16[2,384,512]{2,1,0:T(8,128)(2,1)}, bf16[2,384,512]{2,1,0:T(8,128)(2,1)}, u32[]{:S(2)}, u32[]{:S(2)}) collective-permute-start(bf16[2,384,512]{2,1,0:T(8,128)(2,1)} %slice.90), channel_id=1, source_target_pairs={{0,6},{2,0},{4,2},{6,4},{8,14},{10,8},{12,10},{14,12},{16,22},{18,... | collective-permute-start | bytes 2359304 | tf_op jit(solution)/shard_map/ppermute | solution.py:57
  120.2 24.8 %collective-permute-start.14 = (bf16[2,384,512]{2,1,0:T(8,128)(2,1)}, bf16[2,384,512]{2,1,0:T(8,128)(2,1)S(1)}, u32[]{:S(2)}, u32[]{:S(2)}) collective-permute-start(bf16[2,384,512]{2,1,0:T(8,128)(2,1)} %slice.89), channel_id=1, source_target_pairs={{0,2},{2,4},{4,6},{6,0},{8,10},{10,12},{12,14},{14,8},{16,18},{18,... | collective-permute-start | bytes 2359304 | tf_op jit(solution)/shard_map/ppermute | solution.py:57
  147.6 20.2 %slice-start = ((s8[18874368]{0:T(1024)(128)(4,1)}), s8[2097152]{0:T(1024)(128)(4,1)S(1)}, s32[]{:S(2)}) async-start(s8[18874368]{0:T(1024)(128)(4,1)} %bitcast.64), calls=%async_computation.1 | async-start | bytes 4194304
  147.6 20.2 %slice-start.1 = ((s8[18874368]{0:T(1024)(128)(4,1)}), s8[4194304]{0:T(1024)(128)(4,1)S(1)}, s32[]{:S(2)}) async-start(s8[18874368]{0:T(1024)(128)(4,1)} %bitcast.64), calls=%async_computation.2 | async-start | bytes 8388608
  147.6 20.2 %slice-start.2 = ((s8[18874368]{0:T(1024)(128)(4,1)}), s8[4194304]{0:T(1024)(128)(4,1)S(1)}, s32[]{:S(2)}) async-start(s8[18874368]{0:T(1024)(128)(4,1)} %bitcast.64), calls=%async_computation.3 | async-start | bytes 8388608
  157.6 10.2 %slice-start.3 = ((s8[18874368]{0:T(1024)(128)(4,1)}), s8[4194304]{0:T(1024)(128)(4,1)S(1)}, s32[]{:S(2)}) async-start(s8[18874368]{0:T(1024)(128)(4,1)} %bitcast.64), calls=%async_computation.4 | async-start | bytes 8388608
  157.6 10.2 %slice-start.4 = ((s8[18874368]{0:T(1024)(128)(4,1)}), s8[4194304]{0:T(1024)(128)(4,1)S(1)}, s32[]{:S(2)}) async-start(s8[18874368]{0:T(1024)(128)(4,1)} %bitcast.64), calls=%async_computation.5 | async-start | bytes 8388608
  157.6 10.3 %copy-start.14 = (bf16[64,3072]{1,0:T(8,128)(2,1)S(1)}, bf16[64,3072]{1,0:T(8,128)(2,1)}, u32[]{:S(2)}) copy-start(bf16[64,3072]{1,0:T(8,128)(2,1)} %fusion.10.x_ref) | copy-start | bytes 1179652
  163.0 24.4 %slice-start.5 = ((s8[6291456]{0:T(1024)(128)(4,1)}), s8[4194304]{0:T(1024)(128)(4,1)S(1)}, s32[]{:S(2)}) async-start(s8[6291456]{0:T(1024)(128)(4,1)} %bitcast.72), calls=%async_computation.6 | async-start | bytes 8388608
  167.9 16.3 %copy-start.20 = (bf16[3,64,3072]{2,1,0:T(8,128)(2,1)S(1)}, bf16[3,64,3072]{2,1,0:T(8,128)(2,1)}, u32[]{:S(2)}) copy-start(bf16[3,64,3072]{2,1,0:T(8,128)(2,1)} %param.7) | copy-start | bytes 3538948
  167.9 19.5 %slice-start.6 = ((s8[6291456]{0:T(1024)(128)(4,1)}), s8[2097152]{0:T(1024)(128)(4,1)S(1)}, s32[]{:S(2)}) async-start(s8[6291456]{0:T(1024)(128)(4,1)} %bitcast.72), calls=%async_computation.7 | async-start | bytes 4194304
  172.0 12.2 %collective-permute-start.16 = (bf16[64,3072]{1,0:T(8,128)(2,1)S(1)}, bf16[64,3072]{1,0:T(8,128)(2,1)S(1)}, u32[]{:S(2)}, u32[]{:S(2)}) collective-permute-start(bf16[64,3072]{1,0:T(8,128)(2,1)S(1)} %shard_map.78), channel_id=1, source_target_pairs={{0,32},{32,64},{64,96},{1,33},{33,65},{65,97},{2,34},{34,66},{66,9... | collective-permute-start | bytes 1179656 | tf_op jit(solution)/shard_map/ppermute | solution.py:336
  198.9 12.2 %collective-permute-start.17 = (bf16[64,3072]{1,0:T(8,128)(2,1)S(1)}, bf16[64,3072]{1,0:T(8,128)(2,1)S(1)}, u32[]{:S(2)}, u32[]{:S(2)}) collective-permute-start(bf16[64,3072]{1,0:T(8,128)(2,1)S(1)} %shard_map.80), channel_id=1, source_target_pairs={{0,32},{32,64},{64,96},{1,33},{33,65},{65,97},{2,34},{34,66},{66,9... | collective-permute-start | bytes 1179656 | tf_op jit(solution)/shard_map/ppermute | solution.py:336
  226.1 12.2 %collective-permute-start.18 = (bf16[64,3072]{1,0:T(8,128)(2,1)S(1)}, bf16[64,3072]{1,0:T(8,128)(2,1)S(1)}, u32[]{:S(2)}, u32[]{:S(2)}) collective-permute-start(bf16[64,3072]{1,0:T(8,128)(2,1)S(1)} %shard_map.82), channel_id=1, source_target_pairs={{0,32},{32,64},{64,96},{1,33},{33,65},{65,97},{2,34},{34,66},{66,9... | collective-permute-start | bytes 1179656 | tf_op jit(solution)/shard_map/ppermute | solution.py:336
  252.9 12.2 %collective-permute-start.19 = (bf16[64,3072]{1,0:T(8,128)(2,1)S(1)}, bf16[64,3072]{1,0:T(8,128)(2,1)S(1)}, u32[]{:S(2)}, u32[]{:S(2)}) collective-permute-start(bf16[64,3072]{1,0:T(8,128)(2,1)S(1)} %shard_map.84), channel_id=1, source_target_pairs={{0,32},{32,64},{64,96},{1,33},{33,65},{65,97},{2,34},{34,66},{66,9... | collective-permute-start | bytes 1179656 | tf_op jit(solution)/shard_map/ppermute | solution.py:336
  280.0 12.2 %collective-permute-start.20 = (bf16[64,3072]{1,0:T(8,128)(2,1)S(1)}, bf16[64,3072]{1,0:T(8,128)(2,1)S(1)}, u32[]{:S(2)}, u32[]{:S(2)}) collective-permute-start(bf16[64,3072]{1,0:T(8,128)(2,1)S(1)} %shard_map.86), channel_id=1, source_target_pairs={{0,32},{32,64},{64,96},{1,33},{33,65},{65,97},{2,34},{34,66},{66,9... | collective-permute-start | bytes 1179656 | tf_op jit(solution)/shard_map/ppermute | solution.py:336
  (19 other events, 87.7 us)
Sparse Core Ops, SparseCore 0:
  11.0 127.8 all-gather.3

commit v3 on v2

--- a/solution.py
+++ b/solution.py
@@ -64,20 +64,25 @@
     return below, above, shift(below[:half], axis, 1), shift(above[half:], axis, -1)
 
 
+def short_ring(block, axis):
+    below = shift(block, axis, 1)
+    above = shift(block, axis, -1)
+    far = shift(below, axis, 1) if axis == "y" else shift(above, axis, -1)
+    return below, above, far
+
+
 def pack_kernel(axes, place, *refs):
     count = len(axes)
-    ins, outs, sems = refs[: 5 * count], refs[5 * count : 6 * count], refs[-1]
+    ins, outs, sems = refs[: 4 * count], refs[4 * count : 5 * count], refs[-1]
     copies = []
     for group, (axis, slab) in enumerate(zip(axes, outs)):
         at = place[0 if axis == "z" else 1]
-        own, below, above, low, high = ins[5 * group : 5 * group + 5]
-        half = own.shape[0] // 2
+        own, below, above, far = ins[4 * group : 4 * group + 4]
         for src, dst in (
             (own, slab.at[at]),
             (below, slab.at[(at + 3) % SIDE]),
             (above, slab.at[(at + 1) % SIDE]),
-            (low, slab.at[(at + 2) % SIDE, pl.ds(0, half)]),
-            (high, slab.at[(at + 2) % SIDE, pl.ds(half, half)]),
+            (far, slab.at[(at + 2) % SIDE]),
         ):
             copies.append(pltpu.make_async_copy(src, dst, sems.at[len(copies)]))
     for copy in copies:
@@ -91,16 +96,16 @@
     return pl.pallas_call(
         functools.partial(pack_kernel, axes),
         out_shape=[shape] * len(axes),
-        in_specs=[SMEM] + [HBM] * (5 * len(axes)),
+        in_specs=[SMEM] + [HBM] * (4 * len(axes)),
         out_specs=[VMEM] * len(axes),
-        scratch_shapes=[pltpu.SemaphoreType.DMA((5 * len(axes),))],
+        scratch_shapes=[pltpu.SemaphoreType.DMA((4 * len(axes),))],
         compiler_params=pltpu.CompilerParams(vmem_limit_bytes=16 * MIB),
     )(place, *[piece for group in rings for piece in group])
 
 
 def gather(place, blocks):
     firsts = [first for _, first, _ in blocks]
-    slabs = pack(place, firsts, [(b,) + ring(b, first) for b, first, _ in blocks])
+    slabs = pack(place, firsts, [(b,) + short_ring(b, first) for b, first, _ in blocks])
     pieces = []
     for slab, (_, first, column) in zip(slabs, blocks):
         axis = "z" if first == "y" else "y"

time: 316 us -> 319 us (level)
  waiting for transfers between devices: 106 us -> 119 us
  blocking collectives: 44.3 us -> 40.4 us
    ppermute x16 -> x14, waiting for transfers between devices: 56.7 us -> 64.2 us  [shift(): return lax.ppermute(block, 'seq', pairs)]
    all_gather x1, waiting for transfers between devices: 3.87 us -> 9.05 us  [body(): gathered = lax.all_gather(local, 'seq', axis=0)]
    all_gather x6, blocking collectives: 29 us -> 25.7 us  [body(): whole = lax.all_gather(current, 'mp', axis=1, tiled=True)]
    ppermute x16 -> x14, starting transfers between devices: 21.8 us -> 19.2 us  [shift(): return lax.ppermute(block, 'seq', pairs)]
  transfers between devices with their start and end apart: 22 -> 20, of which waited for: 13 -> 12; matrix products, arithmetic and copies ran while one was open for 3% -> 2% of each run, Pallas kernels for 2% -> 2%
where the time goes in v3:
time: 319 us; the launch traced here: 318 us
  waiting for transfers between devices  119 us (37%)
  Pallas kernels  62.8 us (20%)
  blocking collectives  40.4 us (13%)
  local copies, waits for them, and re-layouts  36.3 us (11%)
  starting transfers between devices  34.9 us (11%)
  between operations  19.6 us (6%)
  other arithmetic  5.73 us (2%)
    ppermute x14, waiting for transfers between devices, shift(): return lax.ppermute(block, 'seq', pairs)  64.2 us
    ppermute x5, waiting for transfers between devices, body(): lax.ppermute(mixed, 'segment', [(i, i + 1) for i in range(segments - 1)])  45.3 us
    pallas_call x6, Pallas kernels, attend(): pl.pallas_call(attend_kernel, out_shape=jax.ShapeDtypeStruct((tokens, wid...  31.9 us
    unnamed x68, local copies, waits for them, and re-layouts  25.9 us
    all_gather x6, blocking collectives, body(): whole = lax.all_gather(current, 'mp', axis=1, tiled=True)  25.7 us
    pallas_call x5, Pallas kernels, project(): pl.pallas_call(functools.partial(project_kernel, column), out_shape=jax.S...  20.2 us
    ppermute x14, starting transfers between devices, shift(): return lax.ppermute(block, 'seq', pairs)  19.2 us
    ppermute x5, starting transfers between devices, body(): lax.ppermute(mixed, 'segment', [(i, i + 1) for i in range(segments - 1)])  15.6 us
  transfers between devices with their start and end apart: 20, of which 12 were waited for; matrix products, arithmetic and copies ran while one was open for 2% of the time, Pallas kernels for 2%

profile of v3, /device:TPU:3, one launch (start us, length us, event | category | flops | bytes accessed | tf_op | source)
XLA Modules:
  0.0 318.3 jit_solution(5275514053812651072)
XLA Ops:
  10.9 3.8 %collective-permute-start.4 = (bf16[384,512]{1,0:T(8,128)(2,1)S(1)}, bf16[384,512]{1,0:T(8,128)(2,1)S(1)}, u32[]{:S(2)}, u32[]{:S(2)}) collective-permute-start(bf16[384,512]{1,0:T(8,128)(2,1)S(1)} %get-tuple-element.15.refs_4_), channel_id=1, source_target_pairs={{0,24},{2,26},{4,28},{6,30},{8,0},{10,2},{12,4},{14,6},{16,8},{18,... | collective-permute-start | bytes 1179656 | tf_op jit(solution)/shard_map/ppermute | solution.py:57
  17.4 5.0 %collective-permute-done.4.refs_6_ = bf16[384,512]{1,0:T(8,128)(2,1)S(1)} collective-permute-done((bf16[384,512]{1,0:T(8,128)(2,1)S(1)}, bf16[384,512]{1,0:T(8,128)(2,1)S(1)}, u32[]{:S(2)}, u32[]{:S(2)}) %collective-permute-start.4) | collective-permute-done | bytes 393248 | tf_op jit(solution)/shard_map/ppermute | solution.py:57
  27.3 15.0 %collective-permute-done.5.refs_7_ = bf16[384,512]{1,0:T(8,128)(2,1)S(1)} collective-permute-done((bf16[384,512]{1,0:T(8,128)(2,1)S(1)}, bf16[384,512]{1,0:T(8,128)(2,1)S(1)}, u32[]{:S(2)}, u32[]{:S(2)}) %collective-permute-start.5) | collective-permute-done | bytes 393248 | tf_op jit(solution)/shard_map/ppermute | solution.py:57
  42.3 3.8 %collective-permute-done.2.refs_3_ = bf16[384,512]{1,0:T(8,128)(2,1)S(1)} collective-permute-done((bf16[384,512]{1,0:T(8,128)(2,1)S(1)}, bf16[384,512]{1,0:T(8,128)(2,1)S(1)}, u32[]{:S(2)}, u32[]{:S(2)}) %collective-permute-start.2) | collective-permute-done | bytes 393248 | tf_op jit(solution)/shard_map/ppermute | solution.py:57
  46.1 3.8 %shard_map.74 = (bf16[4,384,512]{2,1,0:T(8,128)(2,1)}, bf16[4,384,512]{2,1,0:T(8,128)(2,1)}) custom-call(s32[2]{0:T(128)S(1)} %pad_add_fusion.place, bf16[384,512]{1,0:T(8,128)(2,1)S(1)} %get-tuple-element.16.refs_0_, bf16[384,512]{1,0:T(8,128)(2,1)S(1)} %collective-permute-done.refs_1_, bf16[384,512]{1,0:T(8,128)(2,1)S(1)} %collective-permute-done.1.refs_2_, ...), custom_call_target="tpu_custom_call" | custom-call | tf_op jit(solution)/shard_map/pallas_call | solution.py:96
  57.4 6.4 %copy-done.7 = bf16[1,3072,3072]{2,1,0:T(8,128)(2,1)S(1)} copy-done((bf16[1,3072,3072]{2,1,0:T(8,128)(2,1)S(1)}, bf16[1,3072,3072]{2,1,0:T(8,128)(2,1)}, u32[]{:S(2)}) %copy-start.7) | copy-done | bytes 18874392
  65.0 6.5 %copy-done.2 = bf16[3072,3072]{1,0:T(8,128)(2,1)} copy-done((bf16[3072,3072]{1,0:T(8,128)(2,1)}, bf16[3072,3072]{1,0:T(8,128)(2,1)S(1)}, u32[]{:S(2)}) %copy-start.2) | copy-done | bytes 18874392
  73.4 38.7 %collective-permute-done.7.refs_2_ = bf16[4,384,512]{2,1,0:T(8,128)(2,1)S(1)} collective-permute-done((bf16[4,384,512]{2,1,0:T(8,128)(2,1)}, bf16[4,384,512]{2,1,0:T(8,128)(2,1)S(1)}, u32[]{:S(2)}, u32[]{:S(2)}) %collective-permute-start.7) | collective-permute-done | bytes 1572896 | tf_op jit(solution)/shard_map/ppermute | solution.py:57
  123.8 9.3 %all-gather = bf16[1,64,6144]{2,1,0:T(8,128)(2,1)} all-gather(bf16[1,64,3072]{2,1,0:T(8,128)(2,1)S(1)} %constant_dynamic-slice_fusion), channel_id=2, replica_groups=mesh['segment'=4,'seq'=16,'mp'=2] {'mp'}, dimensions={2}, use_global_device_ids=true | all-gather | bytes 1179648 | tf_op jit(solution)/shard_map/all_gather | solution.py:336
  133.9 9.1 %all-gather.4.cloned.1.call-done = bf16[10752,512]{1,0:T(8,128)(2,1)} async-done(((bf16[672,512]{1,0:T(8,128)(2,1)}), bf16[10752,512]{1,0:T(8,128)(2,1)}) %all-gather.4.cloned.1.call-update) | async-done | bytes 11010064 | tf_op jit(solution)/shard_map/all_gather | solution.py:318
  142.9 4.1 %copy-done.8 = bf16[10752,512]{1,0:T(8,128)(2,1)S(1)} copy-done((bf16[10752,512]{1,0:T(8,128)(2,1)S(1)}, bf16[10752,512]{1,0:T(8,128)(2,1)}, u32[]{:S(2)}) %copy-start.8) | copy-done | bytes 11010072
  151.7 4.8 %shard_map.75 = bf16[4,4,4,384,256]{4,3,2,1,0:T(8,128)(2,1)S(1)} custom-call(s32[2]{0:T(128)S(1)} %pad_add_fusion.place, bf16[2,16,384,256]{3,2,1,0:T(8,128)(2,1)S(1)} %get-tuple-element.10._.kept_ref, bf16[4,384,512]{2,1,0:T(8,128)(2,1)} %get-tuple-element.11.refs_0_, bf16[4,384,512]{2,1,0:T(8,128)(2,1)S(1)} %copy-done.12, ...), custom_call_target="tpu_custom_call" | custom-call | tf_op jit(solution)/shard_map/pallas_call | solution.py:148
  156.6 3.5 %copy-done.4 = bf16[2,16,384,256]{3,2,1,0:T(8,128)(2,1)S(1)} copy-done((bf16[2,16,384,256]{3,2,1,0:T(8,128)(2,1)S(1)}, bf16[2,16,384,256]{3,2,1,0:T(8,128)(2,1)}, u32[]{:S(2)}) %copy-start.4) | copy-done | bytes 6291480
  161.7 5.4 %shard_map.76 = bf16[64,1536]{1,0:T(8,128)(2,1)S(1)} custom-call(s32[3]{0:T(128)S(1)} %copy-done.18, s32[3]{0:T(128)S(1)} %copy-done.17, s32[1]{0:T(128)} %bitcast.slot, bf16[64,6144]{1,0:T(8,128)(2,1)S(1)} %bitcast.88, bf16[4,16,384,256]{3,2,1,0:T(8,128)(2,1)S(1)} %bitcast.66, bf16[2,16,384,256]{3,2,1,0:T(8,128)(2,1)S(1)} %copy-done.4, ...), custom_call_target="tpu_custom_call" | custom-call | flops 1207959552 | bytes 18874368 | tf_op jit(solution)/shard_map/pallas_call | solution.py:241
  167.1 4.2 %all_gather.45.a_ref = bf16[64,3072]{1,0:T(8,128)(2,1)S(1)} all-gather(bf16[64,1536]{1,0:T(8,128)(2,1)S(1)} %shard_map.76), channel_id=1, replica_groups=mesh['segment'=4,'seq'=16,'mp'=2] {'mp'}, dimensions={1}, use_global_device_ids=true | all-gather | bytes 589824 | tf_op jit(solution)/shard_map/all_gather | solution.py:338
  171.4 4.0 %shard_map.78 = bf16[64,3072]{1,0:T(8,128)(2,1)S(1)} custom-call(bf16[64,3072]{1,0:T(8,128)(2,1)S(1)} %all_gather.45.a_ref, bf16[3072,3072]{1,0:T(8,128)(2,1)S(1)} %bitcast.65, bf16[64,3072]{1,0:T(8,128)(2,1)S(1)} %copy-done.14), custom_call_target="tpu_custom_call" | custom-call | flops 1207959552 | bytes 18874368 | tf_op jit(solution)/shard_map/pallas_call | solution.py:289
  178.6 9.0 %collective-permute-done.14 = bf16[64,3072]{1,0:T(8,128)(2,1)S(1)} collective-permute-done((bf16[64,3072]{1,0:T(8,128)(2,1)S(1)}, bf16[64,3072]{1,0:T(8,128)(2,1)S(1)}, u32[]{:S(2)}, u32[]{:S(2)}) %collective-permute-start.14) | collective-permute-done | bytes 393248 | tf_op jit(solution)/shard_map/ppermute | solution.py:341
  190.9 5.3 %shard_map.79 = bf16[64,1536]{1,0:T(8,128)(2,1)S(1)} custom-call(s32[3]{0:T(128)S(1)} %copy-done.18, s32[3]{0:T(128)S(1)} %copy-done.17, s32[1]{0:T(128)} %bitcast.19.slot, bf16[64,6144]{1,0:T(8,128)(2,1)S(1)} %all_gather.46.x_ref, bf16[4,16,384,256]{3,2,1,0:T(8,128)(2,1)S(1)} %bitcast.67, bf16[2,16,384,256]{3,2,1,0:T(8,128)(2,1)S(1)} %bitcast.73, ...), custom_call_target="tpu_custom_call" | custom-call | flops 1207959552 | bytes 18874368 | tf_op jit(solution)/shard_map/pallas_call | solution.py:241
  198.3 4.0 %shard_map.80 = bf16[64,3072]{1,0:T(8,128)(2,1)S(1)} custom-call(bf16[64,3072]{1,0:T(8,128)(2,1)S(1)} %all_gather.47.a_ref, bf16[3072,3072]{1,0:T(8,128)(2,1)S(1)} %bitcast.65, bf16[64,3072]{1,0:T(8,128)(2,1)S(1)} %bitcast_select_fusion.1.x_ref), custom_call_target="tpu_custom_call" | custom-call | flops 1207959552 | bytes 18874368 | tf_op jit(solution)/shard_map/pallas_call | solution.py:289
  205.5 9.1 %collective-permute-done.15 = bf16[64,3072]{1,0:T(8,128)(2,1)S(1)} collective-permute-done((bf16[64,3072]{1,0:T(8,128)(2,1)S(1)}, bf16[64,3072]{1,0:T(8,128)(2,1)S(1)}, u32[]{:S(2)}, u32[]{:S(2)}) %collective-permute-start.15) | collective-permute-done | bytes 393248 | tf_op jit(solution)/shard_map/ppermute | solution.py:341
  218.0 5.3 %shard_map.81 = bf16[64,1536]{1,0:T(8,128)(2,1)S(1)} custom-call(s32[3]{0:T(128)S(1)} %copy-done.18, s32[3]{0:T(128)S(1)} %copy-done.17, s32[1]{0:T(128)} %bitcast.23.slot, bf16[64,6144]{1,0:T(8,128)(2,1)S(1)} %all_gather.48.x_ref, bf16[4,16,384,256]{3,2,1,0:T(8,128)(2,1)S(1)} %bitcast.68, bf16[2,16,384,256]{3,2,1,0:T(8,128)(2,1)S(1)} %bitcast.73, ...), custom_call_target="tpu_custom_call" | custom-call | flops 1207959552 | bytes 18874368 | tf_op jit(solution)/shard_map/pallas_call | solution.py:241
  225.4 4.0 %shard_map.82 = bf16[64,3072]{1,0:T(8,128)(2,1)S(1)} custom-call(bf16[64,3072]{1,0:T(8,128)(2,1)S(1)} %all_gather.49.a_ref, bf16[3072,3072]{1,0:T(8,128)(2,1)S(1)} %bitcast.65, bf16[64,3072]{1,0:T(8,128)(2,1)S(1)} %bitcast_select_fusion.x_ref), custom_call_target="tpu_custom_call" | custom-call | flops 1207959552 | bytes 18874368 | tf_op jit(solution)/shard_map/pallas_call | solution.py:289
  232.7 9.1 %collective-permute-done.16.x_ref = bf16[64,3072]{1,0:T(8,128)(2,1)S(1)} collective-permute-done((bf16[64,3072]{1,0:T(8,128)(2,1)S(1)}, bf16[64,3072]{1,0:T(8,128)(2,1)S(1)}, u32[]{:S(2)}, u32[]{:S(2)}) %collective-permute-start.16) | collective-permute-done | bytes 393248 | tf_op jit(solution)/shard_map/ppermute | solution.py:341
  244.9 5.3 %shard_map.83 = bf16[64,1536]{1,0:T(8,128)(2,1)S(1)} custom-call(s32[3]{0:T(128)S(1)} %copy-done.18, s32[3]{0:T(128)S(1)} %copy-done.17, s32[1]{0:T(128)} %bitcast.27.slot, bf16[64,6144]{1,0:T(8,128)(2,1)S(1)} %all_gather.50.x_ref, bf16[4,16,384,256]{3,2,1,0:T(8,128)(2,1)S(1)} %bitcast.69, bf16[2,16,384,256]{3,2,1,0:T(8,128)(2,1)S(1)} %bitcast.73, ...), custom_call_target="tpu_custom_call" | custom-call | flops 1207959552 | bytes 18874368 | tf_op jit(solution)/shard_map/pallas_call | solution.py:241
  252.3 4.0 %shard_map.84 = bf16[64,3072]{1,0:T(8,128)(2,1)S(1)} custom-call(bf16[64,3072]{1,0:T(8,128)(2,1)S(1)} %all_gather.51.a_ref, bf16[3072,3072]{1,0:T(8,128)(2,1)S(1)} %bitcast.65, bf16[64,3072]{1,0:T(8,128)(2,1)S(1)} %collective-permute-done.16.x_ref), custom_call_target="tpu_custom_call" | custom-call | flops 1207959552 | bytes 18874368 | tf_op jit(solution)/shard_map/pallas_call | solution.py:289
  259.5 9.1 %collective-permute-done.17.x_ref = bf16[64,3072]{1,0:T(8,128)(2,1)S(1)} collective-permute-done((bf16[64,3072]{1,0:T(8,128)(2,1)S(1)}, bf16[64,3072]{1,0:T(8,128)(2,1)S(1)}, u32[]{:S(2)}, u32[]{:S(2)}) %collective-permute-start.17) | collective-permute-done | bytes 393248 | tf_op jit(solution)/shard_map/ppermute | solution.py:341
  268.6 3.4 %all_gather.52.x_ref = bf16[64,6144]{1,0:T(8,128)(2,1)S(1)} all-gather(bf16[64,3072]{1,0:T(8,128)(2,1)S(1)} %collective-permute-done.17.x_ref), channel_id=1, replica_groups=mesh['segment'=4,'seq'=16,'mp'=2] {'mp'}, dimensions={1}, use_global_device_ids=true | all-gather | bytes 1179648 | tf_op jit(solution)/shard_map/all_gather | solution.py:336
  272.0 5.3 %shard_map.85 = bf16[64,1536]{1,0:T(8,128)(2,1)S(1)} custom-call(s32[3]{0:T(128)S(1)} %copy-done.18, s32[3]{0:T(128)S(1)} %copy-done.17, s32[1]{0:T(128)} %bitcast.29.slot, bf16[64,6144]{1,0:T(8,128)(2,1)S(1)} %all_gather.52.x_ref, bf16[4,16,384,256]{3,2,1,0:T(8,128)(2,1)S(1)} %bitcast.70, bf16[2,16,384,256]{3,2,1,0:T(8,128)(2,1)S(1)} %bitcast.73, ...), custom_call_target="tpu_custom_call" | custom-call | flops 1207959552 | bytes 18874368 | tf_op jit(solution)/shard_map/pallas_call | solution.py:241
  279.4 4.0 %shard_map.86 = bf16[64,3072]{1,0:T(8,128)(2,1)S(1)} custom-call(bf16[64,3072]{1,0:T(8,128)(2,1)S(1)} %all_gather.53.a_ref, bf16[3072,3072]{1,0:T(8,128)(2,1)S(1)} %bitcast.65, bf16[64,3072]{1,0:T(8,128)(2,1)S(1)} %collective-permute-done.17.x_ref), custom_call_target="tpu_custom_call" | custom-call | flops 1207959552 | bytes 18874368 | tf_op jit(solution)/shard_map/pallas_call | solution.py:289
  286.6 9.1 %collective-permute-done.18 = bf16[64,3072]{1,0:T(8,128)(2,1)S(1)} collective-permute-done((bf16[64,3072]{1,0:T(8,128)(2,1)S(1)}, bf16[64,3072]{1,0:T(8,128)(2,1)S(1)}, u32[]{:S(2)}, u32[]{:S(2)}) %collective-permute-start.18) | collective-permute-done | bytes 393248 | tf_op jit(solution)/shard_map/ppermute | solution.py:341
  298.9 5.3 %shard_map.87 = bf16[64,1536]{1,0:T(8,128)(2,1)S(1)} custom-call(s32[3]{0:T(128)S(1)} %copy-done.18, s32[3]{0:T(128)S(1)} %copy-done.17, s32[1]{0:T(128)} %bitcast.31.slot, bf16[64,6144]{1,0:T(8,128)(2,1)S(1)} %all_gather.54.x_ref, bf16[4,16,384,256]{3,2,1,0:T(8,128)(2,1)S(1)} %bitcast.71, bf16[2,16,384,256]{3,2,1,0:T(8,128)(2,1)S(1)} %bitcast.73, ...), custom_call_target="tpu_custom_call" | custom-call | flops 1207959552 | bytes 18874368 | tf_op jit(solution)/shard_map/pallas_call | solution.py:241
  306.3 4.0 %shard_map.88 = bf16[6,64,3072]{2,1,0:T(8,128)(2,1)S(1)} fusion(bf16[6,64,3072]{2,1,0:T(8,128)(2,1)S(1)} %bitcast_dynamic-update-slice_fusion.1, bf16[64,3072]{1,0:T(8,128)(2,1)S(1)} %all_gather.55, bf16[3072,3072]{1,0:T(8,128)(2,1)S(1)} %bitcast.65, bf16[64,3072]{1,0:T(8,128)(2,1)S(1)} %collective-permute-done.18), kind=kCustom, calls=%fused_computation.4 | custom fusion | flops 1207959552 | bytes 20054016 | tf_op jit(solution)/shard_map/pallas_call | solution.py:289
  (123 shorter events, 75.9 us)
Async XLA Ops:
  6.5 136.4 %all-gather.4.cloned.1.call-start = ((), (), s32[]{:S(2)}) async-start(), calls=%async_computation | async-start | bytes 11698176 | tf_op jit(solution)/shard_map/all_gather | solution.py:318
  9.9 43.0 %copy-start.17 = (s32[3]{0:T(128)S(1)}, s32[3]{0:T(128)}, u32[]{:S(2)}) copy-start(s32[3]{0:T(128)} %order.11) | copy-start | bytes 40
  10.9 11.6 %collective-permute-start.4 = (bf16[384,512]{1,0:T(8,128)(2,1)S(1)}, bf16[384,512]{1,0:T(8,128)(2,1)S(1)}, u32[]{:S(2)}, u32[]{:S(2)}) collective-permute-start(bf16[384,512]{1,0:T(8,128)(2,1)S(1)} %get-tuple-element.15.refs_4_), channel_id=1, source_target_pairs={{0,24},{2,26},{4,28},{6,30},{8,0},{10,2},{12,4},{14,6},{16,8},{18,... | collective-permute-start | bytes 1179656 | tf_op jit(solution)/shard_map/ppermute | solution.py:57
  14.7 11.2 %collective-permute-start = (bf16[384,512]{1,0:T(8,128)(2,1)S(1)}, bf16[384,512]{1,0:T(8,128)(2,1)S(1)}, u32[]{:S(2)}, u32[]{:S(2)}) collective-permute-start(bf16[384,512]{1,0:T(8,128)(2,1)S(1)} %get-tuple-element.16.refs_0_), channel_id=1, source_target_pairs={{0,2},{2,4},{4,6},{6,0},{8,10},{10,12},{12,14},{14,8},{16,18},{18,... | collective-permute-start | bytes 1179656 | tf_op jit(solution)/shard_map/ppermute | solution.py:57
  16.0 11.3 %collective-permute-start.3 = (bf16[384,512]{1,0:T(8,128)(2,1)S(1)}, bf16[384,512]{1,0:T(8,128)(2,1)S(1)}, u32[]{:S(2)}, u32[]{:S(2)}) collective-permute-start(bf16[384,512]{1,0:T(8,128)(2,1)S(1)} %get-tuple-element.15.refs_4_), channel_id=1, source_target_pairs={{0,8},{2,10},{4,12},{6,14},{8,16},{10,18},{12,20},{14,22},{16,24},... | collective-permute-start | bytes 1179656 | tf_op jit(solution)/shard_map/ppermute | solution.py:57
  16.0 11.3 %collective-permute-start.1 = (bf16[384,512]{1,0:T(8,128)(2,1)S(1)}, bf16[384,512]{1,0:T(8,128)(2,1)S(1)}, u32[]{:S(2)}, u32[]{:S(2)}) collective-permute-start(bf16[384,512]{1,0:T(8,128)(2,1)S(1)} %get-tuple-element.16.refs_0_), channel_id=1, source_target_pairs={{0,6},{2,0},{4,2},{6,4},{8,14},{10,8},{12,10},{14,12},{16,22},{18,... | collective-permute-start | bytes 1179656 | tf_op jit(solution)/shard_map/ppermute | solution.py:57
  22.5 19.8 %collective-permute-start.5 = (bf16[384,512]{1,0:T(8,128)(2,1)S(1)}, bf16[384,512]{1,0:T(8,128)(2,1)S(1)}, u32[]{:S(2)}, u32[]{:S(2)}) collective-permute-start(bf16[384,512]{1,0:T(8,128)(2,1)S(1)} %collective-permute-done.4.refs_6_), channel_id=1, source_target_pairs={{0,24},{2,26},{4,28},{6,30},{8,0},{10,2},{12,4},{14,6},{16,8},{18,... | collective-permute-start | bytes 1179656 | tf_op jit(solution)/shard_map/ppermute | solution.py:57
  25.9 20.2 %collective-permute-start.2 = (bf16[384,512]{1,0:T(8,128)(2,1)S(1)}, bf16[384,512]{1,0:T(8,128)(2,1)S(1)}, u32[]{:S(2)}, u32[]{:S(2)}) collective-permute-start(bf16[384,512]{1,0:T(8,128)(2,1)S(1)} %collective-permute-done.refs_1_), channel_id=1, source_target_pairs={{0,2},{2,4},{4,6},{6,0},{8,10},{10,12},{12,14},{14,8},{16,18},{18,... | collective-permute-start | bytes 1179656 | tf_op jit(solution)/shard_map/ppermute | solution.py:57
  49.9 62.3 %collective-permute-start.7 = (bf16[4,384,512]{2,1,0:T(8,128)(2,1)}, bf16[4,384,512]{2,1,0:T(8,128)(2,1)S(1)}, u32[]{:S(2)}, u32[]{:S(2)}) collective-permute-start(bf16[4,384,512]{2,1,0:T(8,128)(2,1)} %get-tuple-element.11.refs_0_), channel_id=1, source_target_pairs={{0,24},{2,26},{4,28},{6,30},{8,0},{10,2},{12,4},{14,6},{16,8},{18,... | collective-permute-start | bytes 4718600 | tf_op jit(solution)/shard_map/ppermute | solution.py:57
  49.9 63.3 %collective-permute-start.6 = (bf16[4,384,512]{2,1,0:T(8,128)(2,1)}, bf16[4,384,512]{2,1,0:T(8,128)(2,1)S(1)}, u32[]{:S(2)}, u32[]{:S(2)}) collective-permute-start(bf16[4,384,512]{2,1,0:T(8,128)(2,1)} %get-tuple-element.11.refs_0_), channel_id=1, source_target_pairs={{0,8},{2,10},{4,12},{6,14},{8,16},{10,18},{12,20},{14,22},{16,24},... | collective-permute-start | bytes 4718600 | tf_op jit(solution)/shard_map/ppermute | solution.py:57
  51.4 64.8 %collective-permute-start.11 = (bf16[4,384,512]{2,1,0:T(8,128)(2,1)}, bf16[4,384,512]{2,1,0:T(8,128)(2,1)}, u32[]{:S(2)}, u32[]{:S(2)}) collective-permute-start(bf16[4,384,512]{2,1,0:T(8,128)(2,1)} %get-tuple-element.12.refs_5_), channel_id=1, source_target_pairs={{0,6},{2,0},{4,2},{6,4},{8,14},{10,8},{12,10},{14,12},{16,22},{18,... | collective-permute-start | bytes 4718600 | tf_op jit(solution)/shard_map/ppermute | solution.py:57
  52.7 69.0 %collective-permute-start.10 = (bf16[4,384,512]{2,1,0:T(8,128)(2,1)}, bf16[4,384,512]{2,1,0:T(8,128)(2,1)}, u32[]{:S(2)}, u32[]{:S(2)}) collective-permute-start(bf16[4,384,512]{2,1,0:T(8,128)(2,1)} %get-tuple-element.12.refs_5_), channel_id=1, source_target_pairs={{0,2},{2,4},{4,6},{6,0},{8,10},{10,12},{12,14},{14,8},{16,18},{18,... | collective-permute-start | bytes 4718600 | tf_op jit(solution)/shard_map/ppermute | solution.py:57
  113.2 10.6 %copy-start.19 = (bf16[3,64,3072]{2,1,0:T(8,128)(2,1)S(1)}, bf16[3,64,3072]{2,1,0:T(8,128)(2,1)}, u32[]{:S(2)}) copy-start(bf16[3,64,3072]{2,1,0:T(8,128)(2,1)} %param.7) | copy-start | bytes 3538948
  113.2 34.7 %collective-permute-start.9 = (bf16[2,384,512]{2,1,0:T(8,128)(2,1)}, bf16[2,384,512]{2,1,0:T(8,128)(2,1)}, u32[]{:S(2)}, u32[]{:S(2)}) collective-permute-start(bf16[2,384,512]{2,1,0:T(8,128)(2,1)} %slice.68), channel_id=1, source_target_pairs={{0,24},{2,26},{4,28},{6,30},{8,0},{10,2},{12,4},{14,6},{16,8},{18,... | collective-permute-start | bytes 2359304 | tf_op jit(solution)/shard_map/ppermute | solution.py:57
  113.2 10.5 %copy-start.11 = (bf16[4,384,512]{2,1,0:T(8,128)(2,1)}, bf16[4,384,512]{2,1,0:T(8,128)(2,1)S(1)}, u32[]{:S(2)}) copy-start(bf16[4,384,512]{2,1,0:T(8,128)(2,1)S(1)} %collective-permute-done.6.refs_1_) | copy-start | bytes 4718596
  114.1 33.8 %collective-permute-start.8 = (bf16[2,384,512]{2,1,0:T(8,128)(2,1)}, bf16[2,384,512]{2,1,0:T(8,128)(2,1)}, u32[]{:S(2)}, u32[]{:S(2)}) collective-permute-start(bf16[2,384,512]{2,1,0:T(8,128)(2,1)} %slice.67), channel_id=1, source_target_pairs={{0,8},{2,10},{4,12},{6,14},{8,16},{10,18},{12,20},{14,22},{16,24},... | collective-permute-start | bytes 2359304 | tf_op jit(solution)/shard_map/ppermute | solution.py:57
  118.2 29.7 %collective-permute-start.13 = (bf16[2,384,512]{2,1,0:T(8,128)(2,1)}, bf16[2,384,512]{2,1,0:T(8,128)(2,1)}, u32[]{:S(2)}, u32[]{:S(2)}) collective-permute-start(bf16[2,384,512]{2,1,0:T(8,128)(2,1)} %slice.70), channel_id=1, source_target_pairs={{0,6},{2,0},{4,2},{6,4},{8,14},{10,8},{12,10},{14,12},{16,22},{18,... | collective-permute-start | bytes 2359304 | tf_op jit(solution)/shard_map/ppermute | solution.py:57
  123.7 25.4 %collective-permute-start.12 = (bf16[2,384,512]{2,1,0:T(8,128)(2,1)}, bf16[2,384,512]{2,1,0:T(8,128)(2,1)S(1)}, u32[]{:S(2)}, u32[]{:S(2)}) collective-permute-start(bf16[2,384,512]{2,1,0:T(8,128)(2,1)} %slice.69), channel_id=1, source_target_pairs={{0,2},{2,4},{4,6},{6,0},{8,10},{10,12},{12,14},{14,8},{16,18},{18,... | collective-permute-start | bytes 2359304 | tf_op jit(solution)/shard_map/ppermute | solution.py:57
  151.7 19.6 %slice-start = ((s8[18874368]{0:T(1024)(128)(4,1)}), s8[2097152]{0:T(1024)(128)(4,1)S(1)}, s32[]{:S(2)}) async-start(s8[18874368]{0:T(1024)(128)(4,1)} %bitcast.64), calls=%async_computation.1 | async-start | bytes 4194304
  151.7 19.6 %slice-start.1 = ((s8[18874368]{0:T(1024)(128)(4,1)}), s8[4194304]{0:T(1024)(128)(4,1)S(1)}, s32[]{:S(2)}) async-start(s8[18874368]{0:T(1024)(128)(4,1)} %bitcast.64), calls=%async_computation.2 | async-start | bytes 8388608
  151.7 19.6 %slice-start.2 = ((s8[18874368]{0:T(1024)(128)(4,1)}), s8[4194304]{0:T(1024)(128)(4,1)S(1)}, s32[]{:S(2)}) async-start(s8[18874368]{0:T(1024)(128)(4,1)} %bitcast.64), calls=%async_computation.3 | async-start | bytes 8388608
  161.7 9.6 %slice-start.3 = ((s8[18874368]{0:T(1024)(128)(4,1)}), s8[4194304]{0:T(1024)(128)(4,1)S(1)}, s32[]{:S(2)}) async-start(s8[18874368]{0:T(1024)(128)(4,1)} %bitcast.64), calls=%async_computation.4 | async-start | bytes 8388608
  161.7 9.6 %slice-start.4 = ((s8[18874368]{0:T(1024)(128)(4,1)}), s8[4194304]{0:T(1024)(128)(4,1)S(1)}, s32[]{:S(2)}) async-start(s8[18874368]{0:T(1024)(128)(4,1)} %bitcast.64), calls=%async_computation.5 | async-start | bytes 8388608
  161.7 9.6 %copy-start.14 = (bf16[64,3072]{1,0:T(8,128)(2,1)S(1)}, bf16[64,3072]{1,0:T(8,128)(2,1)}, u32[]{:S(2)}) copy-start(bf16[64,3072]{1,0:T(8,128)(2,1)} %fusion.10.x_ref) | copy-start | bytes 1179652
  167.1 23.8 %slice-start.5 = ((s8[6291456]{0:T(1024)(128)(4,1)}), s8[4194304]{0:T(1024)(128)(4,1)S(1)}, s32[]{:S(2)}) async-start(s8[6291456]{0:T(1024)(128)(4,1)} %bitcast.72), calls=%async_computation.6 | async-start | bytes 8388608
  171.3 16.3 %copy-start.20 = (bf16[3,64,3072]{2,1,0:T(8,128)(2,1)S(1)}, bf16[3,64,3072]{2,1,0:T(8,128)(2,1)}, u32[]{:S(2)}) copy-start(bf16[3,64,3072]{2,1,0:T(8,128)(2,1)} %param.7) | copy-start | bytes 3538948
  171.3 19.5 %slice-start.6 = ((s8[6291456]{0:T(1024)(128)(4,1)}), s8[2097152]{0:T(1024)(128)(4,1)S(1)}, s32[]{:S(2)}) async-start(s8[6291456]{0:T(1024)(128)(4,1)} %bitcast.72), calls=%async_computation.7 | async-start | bytes 4194304
  175.4 12.2 %collective-permute-start.14 = (bf16[64,3072]{1,0:T(8,128)(2,1)S(1)}, bf16[64,3072]{1,0:T(8,128)(2,1)S(1)}, u32[]{:S(2)}, u32[]{:S(2)}) collective-permute-start(bf16[64,3072]{1,0:T(8,128)(2,1)S(1)} %shard_map.78), channel_id=1, source_target_pairs={{0,32},{32,64},{64,96},{1,33},{33,65},{65,97},{2,34},{34,66},{66,9... | collective-permute-start | bytes 1179656 | tf_op jit(solution)/shard_map/ppermute | solution.py:341
  202.3 12.2 %collective-permute-start.15 = (bf16[64,3072]{1,0:T(8,128)(2,1)S(1)}, bf16[64,3072]{1,0:T(8,128)(2,1)S(1)}, u32[]{:S(2)}, u32[]{:S(2)}) collective-permute-start(bf16[64,3072]{1,0:T(8,128)(2,1)S(1)} %shard_map.80), channel_id=1, source_target_pairs={{0,32},{32,64},{64,96},{1,33},{33,65},{65,97},{2,34},{34,66},{66,9... | collective-permute-start | bytes 1179656 | tf_op jit(solution)/shard_map/ppermute | solution.py:341
  229.5 12.2 %collective-permute-start.16 = (bf16[64,3072]{1,0:T(8,128)(2,1)S(1)}, bf16[64,3072]{1,0:T(8,128)(2,1)S(1)}, u32[]{:S(2)}, u32[]{:S(2)}) collective-permute-start(bf16[64,3072]{1,0:T(8,128)(2,1)S(1)} %shard_map.82), channel_id=1, source_target_pairs={{0,32},{32,64},{64,96},{1,33},{33,65},{65,97},{2,34},{34,66},{66,9... | collective-permute-start | bytes 1179656 | tf_op jit(solution)/shard_map/ppermute | solution.py:341
  256.3 12.2 %collective-permute-start.17 = (bf16[64,3072]{1,0:T(8,128)(2,1)S(1)}, bf16[64,3072]{1,0:T(8,128)(2,1)S(1)}, u32[]{:S(2)}, u32[]{:S(2)}) collective-permute-start(bf16[64,3072]{1,0:T(8,128)(2,1)S(1)} %shard_map.84), channel_id=1, source_target_pairs={{0,32},{32,64},{64,96},{1,33},{33,65},{65,97},{2,34},{34,66},{66,9... | collective-permute-start | bytes 1179656 | tf_op jit(solution)/shard_map/ppermute | solution.py:341
  283.5 12.2 %collective-permute-start.18 = (bf16[64,3072]{1,0:T(8,128)(2,1)S(1)}, bf16[64,3072]{1,0:T(8,128)(2,1)S(1)}, u32[]{:S(2)}, u32[]{:S(2)}) collective-permute-start(bf16[64,3072]{1,0:T(8,128)(2,1)S(1)} %shard_map.86), channel_id=1, source_target_pairs={{0,32},{32,64},{64,96},{1,33},{33,65},{65,97},{2,34},{34,66},{66,9... | collective-permute-start | bytes 1179656 | tf_op jit(solution)/shard_map/ppermute | solution.py:341
  (17 other events, 71.3 us)
Sparse Core Ops, SparseCore 0:
  11.0 131.8 all-gather.3
